TPU v7x, 32 devices: a whole 2x2x4 slice. The times are simulated.
32 devices in a mesh: stream: 8 (over z, y), rep: 4 (over x, core).
Axes of the slice: x: 2, y: 2, z: 4, core: 2. Of those that a mesh axis runs over, the one named last changes fastest.
Arguments:
- queries: bfloat16 [4, 1024, 768], P('rep', 'stream'), may hold values from -6 to 6
- memory: bfloat16 [4, 8192, 768], P('rep', 'stream'), may hold values from -6 to 6
- routes: int32 [4, 64], P('rep', 'stream'), may hold values from 0 to 7, as said below
- w_self: bfloat16 [768, 2304], replicated, may hold values from -0.21875 to 0.21875
- w_self_out: bfloat16 [768, 768], replicated, may hold values from -2.5 to 2.5
- w_cross_q: bfloat16 [768, 768], replicated, may hold values from -0.21875 to 0.21875
- w_cross_kv: bfloat16 [768, 1536], replicated, may hold values from -0.21875 to 0.21875
- w_cross_out: bfloat16 [768, 768], replicated, may hold values from -3.5 to 3.5
- w_up: bfloat16 [768, 3072], replicated, may hold values from -0.21875 to 0.21875
- b_up: bfloat16 [3072], replicated, may hold values from -1.5 to 1.5
- w_down: bfloat16 [3072, 768], replicated, may hold values from -0.109375 to 0.109375
- b_down: bfloat16 [768], replicated, may hold values from -1.5 to 1.5
- gain_one: bfloat16 [768], replicated, may hold values from 0.5 to 1.5
- shift_one: bfloat16 [768], replicated, may hold values from -1.5 to 1.5
- gain_two: bfloat16 [768], replicated, may hold values from 0.5 to 1.5
- shift_two: bfloat16 [768], replicated, may hold values from -1.5 to 1.5
- gain_three: bfloat16 [768], replicated, may hold values from 0.5 to 1.5
- shift_three: bfloat16 [768], replicated, may hold values from -1.5 to 1.5
- cotangent: bfloat16 [4, 1024, 768], P('rep', 'stream'), may hold values from -6 to 6
Outputs:
- layer_out: bfloat16 [4, 1024, 768], P('rep', 'stream')
- d_queries: float32 [4, 1024, 768], P('rep', 'stream')
- d_memory: bfloat16 [4, 8192, 768], P('rep', 'stream')
- d_w_self: float32 [768, 2304], P('stream')
- d_w_self_out: float32 [768, 768], P('stream')
- d_w_cross_q: float32 [768, 768], P('stream')
- d_w_cross_kv: float32 [768, 1536], P('stream')
- d_w_cross_out: float32 [768, 768], P('stream')
- d_w_up: float32 [768, 3072], P('stream')
- d_b_up: float32 [3072], P('stream')
- d_w_down: float32 [3072, 768], P('stream')
- d_b_down: float32 [768], P('stream')
- d_gain_one: float32 [768], P('stream')
- d_shift_one: float32 [768], P('stream')
- d_gain_two: float32 [768], P('stream')
- d_shift_two: float32 [768], P('stream')
- d_gain_three: float32 [768], P('stream')
- d_shift_three: float32 [768], P('stream')
Inputs may be any that keep to these rules, and one draw needn't show every extreme that they name: `routes`: of the 8 blocks of one device, exactly 2 are read by the group of the same index of stream in the same replica, and at most 2 by any one group.
All inputs are finite; a program needn't handle non-finite values.
Results may differ from a plain program's by a relative error of at most 0.025.
Values may be sent and summed in bfloat16 or wider, within the bound.
No kernel may reach another device: no remote copies, remote signals or barrier semaphores. Data moves between devices by JAX's collectives and lax.ppermute only.
A program may use at most 384 MiB of HBM per device.

v0:
```python
import jax
import jax.numpy as jnp
from jax import lax
from jax.sharding import PartitionSpec as P

HEADS = 12
HEAD_DIM = 64
BLK = 128


def matmul(left, right):
    return jnp.dot(left, right, preferred_element_type=jnp.float32)


def product_left(left, right):
    return lax.dot_general(
        left, right, (((0,), (0,)), ((), ())), preferred_element_type=jnp.float32
    )


def product_right(left, right):
    return lax.dot_general(
        left, right, (((1,), (1,)), ((), ())), preferred_element_type=jnp.float32
    )


def layer_norm(rows, gain, shift):
    centred = rows - jnp.mean(rows, axis=-1, keepdims=True)
    spread = jnp.mean(centred * centred, axis=-1, keepdims=True)
    return centred * lax.rsqrt(spread + 1e-05) * gain + shift


def split_heads(rows):
    return rows.reshape(rows.shape[0], HEADS, HEAD_DIM).transpose(1, 0, 2)


def join_heads(rows):
    return rows.transpose(1, 0, 2).reshape(rows.shape[1], HEADS * HEAD_DIM)


def masked_scores(query_head, key_head, key_ok):
    scores = product_right(query_head, key_head) * HEAD_DIM ** (-0.5)
    if key_ok is not None:
        scores = jnp.where(key_ok[None, :], scores, -1e30)
    return scores


def attend_forward(query, key_rows, value_rows, key_ok):

    def one_head(item):
        query_head, key_head, value_head = item
        scores = masked_scores(query_head, key_head, key_ok)
        row_max = jnp.max(scores, axis=1, keepdims=True)
        exponent = jnp.exp(scores - row_max)
        row_total = jnp.sum(exponent, axis=1, keepdims=True)
        probability = (exponent / row_total).astype(jnp.bfloat16)
        return (matmul(probability, value_head), (row_max + jnp.log(row_total))[:, 0])

    mixed, log_total = lax.map(
        one_head, (split_heads(query), split_heads(key_rows), split_heads(value_rows))
    )
    return (join_heads(mixed), log_total)


def attend_backward(query, key_rows, value_rows, key_ok, log_total, d_mixed):
    factor = HEAD_DIM ** (-0.5)

    def one_head(item):
        query_head, key_head, value_head, total_head, grad_head = item
        scores = masked_scores(query_head, key_head, key_ok)
        probability = jnp.exp(scores - total_head[:, None])
        d_prob = product_right(grad_head, value_head)
        d_scores = probability * (d_prob - jnp.sum(d_prob * probability, axis=1, keepdims=True))
        d_scores = d_scores.astype(jnp.bfloat16)
        d_query = matmul(d_scores, key_head) * factor
        d_key = product_left(d_scores, query_head) * factor
        d_value = product_left(probability.astype(jnp.bfloat16), grad_head)
        return (d_query, d_key, d_value)

    d_query, d_key, d_value = lax.map(
        one_head,
        (
            split_heads(query),
            split_heads(key_rows),
            split_heads(value_rows),
            log_total,
            split_heads(d_mixed),
        ),
    )
    return (join_heads(d_query), join_heads(d_key), join_heads(d_value))


def on_device(
    queries,
    memory,
    routes,
    w_self,
    w_self_out,
    w_cross_q,
    w_cross_kv,
    w_cross_out,
    w_up,
    b_up,
    w_down,
    b_down,
    gain_one,
    shift_one,
    gain_two,
    shift_two,
    gain_three,
    shift_three,
    cotangent,
):
    streams = lax.axis_size("stream")
    blocks = routes.shape[1]
    capacity = max(2, 2 * blocks // streams)
    slot_count = streams * capacity
    model_width = w_self_out.shape[0]
    target = routes[0]
    hit_table = (target[:, None] == jnp.arange(streams, dtype=jnp.int32)[None, :]).astype(jnp.int32)
    before = jnp.cumsum(hit_table, axis=0) - hit_table
    rank_in = jnp.sum(before * hit_table, axis=1)
    slot_of_block = target * capacity + rank_in
    matched = (slot_of_block[None, :] == jnp.arange(slot_count, dtype=jnp.int32)[:, None]).astype(
        jnp.int32
    )
    block_at = jnp.sum(matched * jnp.arange(blocks, dtype=jnp.int32)[None, :], axis=1)
    live_slot = jnp.sum(matched, axis=1)
    live_grid = live_slot.reshape(streams, capacity)
    filled = (live_slot > 0)[:, None, None]
    nothing = jnp.zeros((), jnp.bfloat16)
    memory_rows = memory[0]
    projected = (
        matmul(memory_rows, w_cross_kv).astype(jnp.bfloat16).reshape(blocks, BLK, 2 * model_width)
    )
    outgoing = jnp.where(filled, jnp.take(projected, block_at, axis=0), nothing)
    arrived, arrived_live = (
        lax.all_to_all(
            outgoing.reshape(streams, capacity, BLK, 2 * model_width),
            "stream",
            split_axis=0,
            concat_axis=0,
            tiled=True,
        ),
        lax.all_to_all(live_grid, "stream", split_axis=0, concat_axis=0, tiled=True),
    )
    keys_values = arrived.reshape(-1, 2 * model_width)
    key_ok = jnp.repeat(arrived_live.reshape(-1), BLK) > 0
    key_cross = keys_values[:, :model_width]
    value_cross = keys_values[:, model_width:]
    gain_a = gain_one.astype(jnp.float32)
    shift_a = shift_one.astype(jnp.float32)
    gain_b = gain_two.astype(jnp.float32)
    shift_b = shift_two.astype(jnp.float32)
    gain_c = gain_three.astype(jnp.float32)
    shift_c = shift_three.astype(jnp.float32)
    tokens = queries[0]
    joined = matmul(tokens, w_self).astype(jnp.bfloat16)
    query_self = joined[:, :model_width]
    key_self = joined[:, model_width : 2 * model_width]
    value_self = joined[:, 2 * model_width :]
    mixed_self, total_self = attend_forward(query_self, key_self, value_self, None)
    mixed_self = mixed_self.astype(jnp.bfloat16)
    residual_one = tokens.astype(jnp.float32) + matmul(mixed_self, w_self_out)
    normed_one = layer_norm(residual_one, gain_a, shift_a).astype(jnp.bfloat16)
    query_cross = matmul(normed_one, w_cross_q).astype(jnp.bfloat16)
    mixed_cross, total_cross = attend_forward(query_cross, key_cross, value_cross, key_ok)
    mixed_cross = mixed_cross.astype(jnp.bfloat16)
    residual_two = normed_one.astype(jnp.float32) + matmul(mixed_cross, w_cross_out)
    normed_two = layer_norm(residual_two, gain_b, shift_b).astype(jnp.bfloat16)
    hidden_pre = matmul(normed_two, w_up) + b_up.astype(jnp.float32)
    hidden = jax.nn.gelu(hidden_pre, approximate=False).astype(jnp.bfloat16)
    residual_three = (
        normed_two.astype(jnp.float32) + matmul(hidden, w_down) + b_down.astype(jnp.float32)
    )
    layer_out = layer_norm(residual_three, gain_c, shift_c).astype(jnp.bfloat16)
    grad_out = cotangent[0].astype(jnp.float32)
    norm_three_pull = jax.vjp(layer_norm, residual_three, gain_c, shift_c)[1]
    d_residual_three, d_gain_c, d_shift_c = norm_three_pull(grad_out)
    d_branch_three = d_residual_three.astype(jnp.bfloat16)
    d_b_down = jnp.sum(d_branch_three.astype(jnp.float32), axis=0)
    d_w_down = product_left(hidden, d_branch_three)
    d_hidden = product_right(d_branch_three, w_down)
    gelu_pull = jax.vjp(lambda value: jax.nn.gelu(value, approximate=False), hidden_pre)[1]
    d_hidden_pre = gelu_pull(d_hidden)[0].astype(jnp.bfloat16)
    d_b_up = jnp.sum(d_hidden_pre.astype(jnp.float32), axis=0)
    d_w_up = product_left(normed_two, d_hidden_pre)
    d_normed_two = d_residual_three + product_right(d_hidden_pre, w_up)
    norm_two_pull = jax.vjp(layer_norm, residual_two, gain_b, shift_b)[1]
    d_residual_two, d_gain_b, d_shift_b = norm_two_pull(d_normed_two)
    d_branch_two = d_residual_two.astype(jnp.bfloat16)
    d_w_cross_out = product_left(mixed_cross, d_branch_two)
    d_mixed_cross = product_right(d_branch_two, w_cross_out).astype(jnp.bfloat16)
    d_query_cross, d_key_cross, d_value_cross = attend_backward(
        query_cross, key_cross, value_cross, key_ok, total_cross, d_mixed_cross
    )
    d_query_cross = d_query_cross.astype(jnp.bfloat16)
    d_keys_values = jnp.concatenate([d_key_cross, d_value_cross], axis=1).astype(jnp.bfloat16)
    d_w_cross_q = product_left(normed_one, d_query_cross)
    d_normed_one = d_residual_two + product_right(d_query_cross, w_cross_q)
    norm_one_pull = jax.vjp(layer_norm, residual_one, gain_a, shift_a)[1]
    d_residual_one, d_gain_a, d_shift_a = norm_one_pull(d_normed_one)
    d_branch_one = d_residual_one.astype(jnp.bfloat16)
    d_w_self_out = product_left(mixed_self, d_branch_one)
    d_mixed_self = product_right(d_branch_one, w_self_out).astype(jnp.bfloat16)
    d_query_self, d_key_self, d_value_self = attend_backward(
        query_self, key_self, value_self, None, total_self, d_mixed_self
    )
    d_joined = jnp.concatenate([d_query_self, d_key_self, d_value_self], axis=1).astype(
        jnp.bfloat16
    )
    d_w_self = product_left(tokens, d_joined)
    d_tokens = d_residual_one + product_right(d_joined, w_self)
    returned = lax.all_to_all(
        d_keys_values.reshape(streams, capacity, BLK, 2 * model_width),
        "stream",
        split_axis=0,
        concat_axis=0,
        tiled=True,
    )
    d_block_rows = jnp.take(
        returned.reshape(slot_count, BLK, 2 * model_width), slot_of_block, axis=0
    ).reshape(-1, 2 * model_width)
    d_w_cross_kv = product_left(memory_rows, d_block_rows)
    d_memory = product_right(d_block_rows, w_cross_kv).astype(jnp.bfloat16)
    gradients = (
        d_w_self,
        d_w_self_out,
        d_w_cross_q,
        d_w_cross_kv,
        d_w_cross_out,
        d_w_up,
        d_b_up,
        d_w_down,
        d_b_down,
        d_gain_a,
        d_shift_a,
        d_gain_b,
        d_shift_b,
        d_gain_c,
        d_shift_c,
    )
    shapes = [item.shape for item in gradients]
    flat = [item.reshape(-1) for item in gradients]
    (
        share_self,
        share_self_out,
        share_cross_q,
        share_cross_kv,
        share_cross_out,
        share_up,
        share_b_up,
        share_down,
        share_b_down,
        share_gain_a,
        share_shift_a,
        share_gain_b,
        share_shift_b,
        share_gain_c,
        share_shift_c,
    ) = (
        lax.psum_scatter(flat[0], "stream", scatter_dimension=0, tiled=True),
        lax.psum_scatter(flat[1], "stream", scatter_dimension=0, tiled=True),
        lax.psum_scatter(flat[2], "stream", scatter_dimension=0, tiled=True),
        lax.psum_scatter(flat[3], "stream", scatter_dimension=0, tiled=True),
        lax.psum_scatter(flat[4], "stream", scatter_dimension=0, tiled=True),
        lax.psum_scatter(flat[5], "stream", scatter_dimension=0, tiled=True),
        lax.psum_scatter(flat[6], "stream", scatter_dimension=0, tiled=True),
        lax.psum_scatter(flat[7], "stream", scatter_dimension=0, tiled=True),
        lax.psum_scatter(flat[8], "stream", scatter_dimension=0, tiled=True),
        lax.psum_scatter(flat[9], "stream", scatter_dimension=0, tiled=True),
        lax.psum_scatter(flat[10], "stream", scatter_dimension=0, tiled=True),
        lax.psum_scatter(flat[11], "stream", scatter_dimension=0, tiled=True),
        lax.psum_scatter(flat[12], "stream", scatter_dimension=0, tiled=True),
        lax.psum_scatter(flat[13], "stream", scatter_dimension=0, tiled=True),
        lax.psum_scatter(flat[14], "stream", scatter_dimension=0, tiled=True),
    )
    summed = (
        lax.psum(share_self.astype(jnp.bfloat16), "rep").astype(jnp.float32),
        lax.psum(share_self_out.astype(jnp.bfloat16), "rep").astype(jnp.float32),
        lax.psum(share_cross_q.astype(jnp.bfloat16), "rep").astype(jnp.float32),
        lax.psum(share_cross_kv.astype(jnp.bfloat16), "rep").astype(jnp.float32),
        lax.psum(share_cross_out.astype(jnp.bfloat16), "rep").astype(jnp.float32),
        lax.psum(share_up.astype(jnp.bfloat16), "rep").astype(jnp.float32),
        lax.psum(share_b_up.astype(jnp.bfloat16), "rep").astype(jnp.float32),
        lax.psum(share_down.astype(jnp.bfloat16), "rep").astype(jnp.float32),
        lax.psum(share_b_down.astype(jnp.bfloat16), "rep").astype(jnp.float32),
        lax.psum(share_gain_a.astype(jnp.bfloat16), "rep").astype(jnp.float32),
        lax.psum(share_shift_a.astype(jnp.bfloat16), "rep").astype(jnp.float32),
        lax.psum(share_gain_b.astype(jnp.bfloat16), "rep").astype(jnp.float32),
        lax.psum(share_shift_b.astype(jnp.bfloat16), "rep").astype(jnp.float32),
        lax.psum(share_gain_c.astype(jnp.bfloat16), "rep").astype(jnp.float32),
        lax.psum(share_shift_c.astype(jnp.bfloat16), "rep").astype(jnp.float32),
    )
    results = [
        part.reshape((shape[0] // streams,) + tuple(shape[1:]))
        for part, shape in zip(summed, shapes)
    ]
    return (
        layer_out[None],
        d_tokens[None],
        d_memory[None],
        results[0],
        results[1],
        results[2],
        results[3],
        results[4],
        results[5],
        results[6],
        results[7],
        results[8],
        results[9],
        results[10],
        results[11],
        results[12],
        results[13],
        results[14],
    )


def solution(mesh):
    in_specs = (
        P("rep", "stream", None),
        P("rep", "stream", None),
        P("rep", "stream"),
        P(),
        P(),
        P(),
        P(),
        P(),
        P(),
        P(),
        P(),
        P(),
        P(),
        P(),
        P(),
        P(),
        P(),
        P(),
        P("rep", "stream", None),
    )
    out_specs = (
        P("rep", "stream", None),
        P("rep", "stream", None),
        P("rep", "stream", None),
        P("stream", None),
        P("stream", None),
        P("stream", None),
        P("stream", None),
        P("stream", None),
        P("stream", None),
        P("stream"),
        P("stream", None),
        P("stream"),
        P("stream"),
        P("stream"),
        P("stream"),
        P("stream"),
        P("stream"),
        P("stream"),
    )
    return jax.shard_map(
        on_device, mesh=mesh, in_specs=in_specs, out_specs=out_specs, check_vma=False
    )
```

profile of v0, /device:TPU:0, one launch (start us, length us, event | category | flops | bytes accessed | tf_op | source)
XLA Modules:
  0.0 2244.3 jit_solution(1979761467448355439)
XLA Ops:
  11.0 7.3 all-to-all-start
  20.8 6.4 convolution_convert_fusion
  27.3 5.5 gather_fusion
  32.8 6.2 select_select_fusion
  38.9 16.2 copy.128
  55.7 6.0 all-to-all-start.1
  77.4 46.3 %while.54 = (s32[]{:T(128)}, bf16[12,128,64]{1,2,0:T(8,128)(2,1)}, f32[12,128]{1,0:T(8,128)}, bf16[12,128,64]{2,1,0:T(8,128)(2,1)}, bf16[12,128,64]{2,1,0:T(8,12...) while((s32[]{:T(128)}, bf16[12,128,64]{1,2,0:T(8,128)(2,1)}, f32[12,128]{1,0:T(8,128)}, ...), condition=%wide.region_3.4_spmd, body=%wide.region_0.3_spmd.sunk | while | flops 4308866 | bytes 334945 | solution.py:59
  147.1 52.2 %all-to-all-done.1 = bf16[8,2,128,1536]{2,1,3,0:T(2,128)(2,1)} async-done(((bf16[8,2,128,1536]{2,1,3,0:T(2,128)(2,1)}), bf16[8,2,128,1536]{2,1,3,0:T(2,128)(2,1)}, u32[]{:S(2)}, u32[]{:S(2)}) %all-to-all-start.1) | async-done | bytes 6291488 | tf_op jit(solution)/shard_map/all_to_all | solution.py:138
  199.4 6.8 copy.129
  206.1 11.1 reshape.434
  217.2 6.7 fusion.123
  223.9 6.6 copy.132
  230.5 6.6 copy.133
  238.4 76.2 %while.56 = (s32[]{:T(128)}, bf16[12,128,64]{1,2,0:T(8,128)(2,1)}, f32[12,128]{1,0:T(8,128)}, bf16[12,128,64]{2,1,0:T(8,128)(2,1)}, bf16[12,2048,64]{2,1,0:T(8,1...) while((s32[]{:T(128)}, bf16[12,128,64]{1,2,0:T(8,128)(2,1)}, ...), condition=%wide.region_13.14_spmd.clone, body=%wide.region_10.13_spmd.clone.sunk | while | flops 69205888 | bytes 4271225 | solution.py:59
  316.9 6.0 multiply_convert_fusion.2
  336.5 118.4 %while.57 = (s32[]{:T(128)}, bf16[12,128,64]{1,2,0:T(8,128)(2,1)}, bf16[12,2048,64]{1,2,0:T(8,128)(2,1)}, bf16[12,2048,64]{1,2,0:T(8,128)(2,1)}, bf16[12,128,64]...) while((s32[]{:T(128)}, bf16[12,128,64]{1,2,0:T(8,128)(2,1)}, ...), condition=%wide.region_24.25_spmd.clone, body=%wide.region_22.24_spmd.clone.sunk | while | flops 170270592 | bytes 10628745 | solution.py:80
  461.8 6.1 concatenate.15
  467.9 8.7 copy.145
  476.6 6.1 concatenate.14
  482.7 8.6 copy.144
  491.4 6.1 pad_maximum_fusion
  504.4 86.1 %while.55 = (s32[]{:T(128)}, bf16[12,128,64]{1,2,0:T(8,128)(2,1)}, bf16[12,128,64]{1,2,0:T(8,128)(2,1)}, bf16[12,128,64]{1,2,0:T(8,128)(2,1)}, bf16[12,128,64]{2...) while((s32[]{:T(128)}, bf16[12,128,64]{1,2,0:T(8,128)(2,1)}, ...), condition=%wide.region_29.30_spmd, body=%wide.region_27.29_spmd.sunk | while | flops 10633090 | bytes 794225 | solution.py:80
  595.7 8.0 copy.146
  603.7 7.9 reshape.443
  633.2 5.8 copy.150
  644.2 10.8 reshape.461
  658.3 5.3 gather_fusion.1
  670.4 6.0 copy.147
  676.5 5.6 reshape.452
  682.1 1440.2 %all-reduce.22 = (bf16[1769472]{0:T(1024)(128)(2,1)}, bf16[589824]{0:T(1024)(128)(2,1)}, bf16[589824]{0:T(1024)(128)(2,1)}, bf16[1179648]{0:T(1024)(128)(2,1)}, ...) all-reduce(f32[1769472]{0:T(1024)} %reshape.443, ...), channel_id=2, replica_groups=mesh['stream'=8,'rep'=4] {'stream'}, use_global_device_ids=true, to_apply=%region_30.31.clone | all-reduce | flops 9445632 | bytes 56673792
  2157.3 7.6 all-reduce.16
  2180.0 48.8 %all-reduce.21.cloned.1.call-done = (bf16[96,2304]{1,0:T(8,128)(2,1)}, bf16[96,768]{1,0:T(8,128)(2,1)}, bf16[96,768]{1,0:T(8,128)(2,1)}, bf16[96,1536]{1,0:T(8,1...) async-done(((bf16[96,2304]{1,0:T(8,128)(2,1)}, bf16[96,768]{1,0:T(8,128)(2,1)}, bf16[96,768]{1,0:T(8,128)(2,1)}, ...) | async-done | bytes 2359312 | tf_op jit(solution)/shard_map/psum | solution.py:279
  (565 shorter events, 499.3 us)
Async XLA Ops:
  7.2 55.7 %copy-start = (bf16[768,2304]{1,0:T(8,128)(2,1)S(1)}, bf16[768,2304]{1,0:T(8,128)(2,1)}, u32[]{:S(2)}) copy-start(bf16[768,2304]{1,0:T(8,128)(2,1)} %param.30) | copy-start | bytes 10616836
  11.0 44.1 %all-to-all-start = ((s32[8,1,2]{2,1,0:T(1,128)}), s32[8,1,2]{2,1,0:T(1,128)S(1)}, u32[]{:S(2)}, u32[]{:S(2)}) async-start(s32[8,1,2]{2,1,0:T(1,128)} %bitcast.36), calls=%async_computation | async-start | bytes 8192 | tf_op jit(solution)/shard_map/all_to_all | solution.py:145
  55.1 6.6 copy-start.40
  55.1 7.2 copy-start.37
  55.7 143.7 %all-to-all-start.1 = ((bf16[8,2,128,1536]{2,1,3,0:T(2,128)(2,1)}), bf16[8,2,128,1536]{2,1,3,0:T(2,128)(2,1)}, u32[]{:S(2)}, u32[]{:S(2)}) async-start(bf16[8,2,128,1536]{2,1,3,0:T(2,128)(2,1)} %copy.128), calls=%async_computation.1 | async-start | bytes 12582912 | tf_op jit(solution)/shard_map/all_to_all | solution.py:138
  65.3 10.8 copy-start.41
  65.3 10.8 copy-start.42
  125.7 4.1 copy-start.21
  125.7 5.9 copy-start.43
  314.6 8.4 slice-start
  316.7 14.8 copy-start.3
  316.7 14.8 copy-start.23
  316.9 14.6 copy-start.34
  316.9 6.1 slice-start.1
  316.9 6.1 copy-start.29
  324.2 4.8 slice-start.2
  454.9 4.0 copy-start.7
  497.5 160.8 %all-to-all-start.2 = ((bf16[8,2,128,1536]{3,2,1,0:T(8,128)(2,1)}), bf16[8,2,128,1536]{3,2,1,0:T(8,128)(2,1)}, u32[]{:S(2)}, u32[]{:S(2)}) async-start(bf16[8,2,128,1536]{3,2,1,0:T(8,128)(2,1)} %pad_maximum_fusion), calls=%async_computation.2 | async-start | bytes 12582912 | tf_op jit(solution)/shard_map/all_to_all | solution.py:214
  502.3 1726.5 %all-reduce.21.cloned.1.call-start = ((), (), s32[]{:S(2)}) async-start(), calls=%async_computation.3 | async-start | bytes 4718592 | tf_op jit(solution)/shard_map/psum | solution.py:279
  633.2 5.8 copy-start.9
  633.2 5.8 copy-start.14
  644.2 10.8 copy-start.45
  658.3 5.3 copy-start.48
  676.5 5.6 copy-start.25
  676.5 5.6 copy-start.26
  676.5 5.6 copy-start.27
  676.5 5.6 copy-start.28
  2145.9 27.7 %copy-start.46 = (pred[1024]{0:T(1024)(128)(4,1)S(1)}, pred[1024]{0:T(1024)(128)(4,1)}, u32[]{:S(2)}) copy-start(pred[1024]{0:T(1024)(128)(4,1)} %broadcast_bitcast_fusion.2) | copy-start | bytes 3076
  2228.8 3.7 copy-start.19
  2228.8 4.5 copy-start.17
  2228.8 5.3 copy-start.18
  2228.8 6.1 copy-start.16
  (30 other events, 55.1 us)
Sparse Core Ops, SparseCore 0:
  2173.8 54.9 all-reduce.20
where the time goes:
time: 2270 us; the launch traced here: 2240 us
  blocking collectives  1450 us (64%)
  matrix products  313 us (14%)
  local copies, waits for them, and re-layouts  281 us (12%)
  waiting for transfers between devices  101 us (4%)
  other arithmetic  63.6 us (3%)
    unnamed x1, blocking collectives  1440 us
    dot_general x55, matrix products, matmul(): return jnp.dot(left, right, preferred_element_type=jnp.float32)  106 us
    dot_general x55, matrix products, product_left(): lax.dot_general(left, right, (((0,), (0,)), ((), ())), preferred_element_...  104 us
    dot_general x79, matrix products, product_right(): lax.dot_general(left, right, (((1,), (1,)), ((), ())), preferred_element_...  103 us
    all_to_all x1, waiting for transfers between devices, on_device(): lax.all_to_all(outgoing.reshape(streams, capacity, BLK, 2 * model_width),...  52.2 us
    psum x1, waiting for transfers between devices, on_device(): lax.psum(share_self.astype(jnp.bfloat16), 'rep').astype(jnp.float32)  48.8 us
    unnamed x136, local copies, waits for them, and re-layouts  48.1 us
  transfers between devices with their start and end apart: 4, of which 2 were waited for; matrix products, arithmetic and copies ran while one was open for 12% of the time, Pallas kernels for 0%

commit v1 on v0

--- a/solution.py
+++ b/solution.py
@@ -1,6 +1,10 @@
+import functools
+
 import jax
 import jax.numpy as jnp
 from jax import lax
+from jax.experimental import pallas as pl
+from jax.experimental.pallas import tpu as pltpu
 from jax.sharding import PartitionSpec as P
 
 HEADS = 12
@@ -318,6 +322,621 @@
     )
 
 
+PAIRS = HEADS // 2
+LANES = 2 * HEAD_DIM
+FACTOR = HEAD_DIM ** (-0.5)
+BF = jnp.bfloat16
+F32 = jnp.float32
+AXES = ("stream", "rep")
+
+
+def whole_in_vmem(count):
+    return [pl.BlockSpec(memory_space=pltpu.VMEM)] * count
+
+
+def local_kernel(body, out_shape, scalars=(), arrays=(), scratch=(), flops=0, limit=52):
+    moved = sum(a.size * a.dtype.itemsize for a in arrays)
+    moved += sum(o.size * o.dtype.itemsize for o in out_shape)
+    return pl.pallas_call(
+        body,
+        out_shape=list(out_shape),
+        in_specs=[pl.BlockSpec(memory_space=pltpu.SMEM)] * len(scalars) + whole_in_vmem(len(arrays)),
+        out_specs=whole_in_vmem(len(out_shape)),
+        scratch_shapes=list(scratch),
+        compiler_params=pltpu.CompilerParams(vmem_limit_bytes=limit * 1024 * 1024),
+        cost_estimate=pl.CostEstimate(flops=flops, bytes_accessed=moved, transcendentals=0),
+    )(*scalars, *arrays)
+
+
+def like(shape, dtype):
+    return jax.ShapeDtypeStruct(shape, dtype)
+
+
+def dot_nn(left, right):
+    return lax.dot_general(left, right, (((1,), (0,)), ((), ())), preferred_element_type=F32)
+
+
+def dot_nt(left, right):
+    return lax.dot_general(left, right, (((1,), (1,)), ((), ())), preferred_element_type=F32)
+
+
+def head_masks(rows):
+    lane = lax.broadcasted_iota(jnp.int32, (rows, LANES), 1)
+    return lane < HEAD_DIM
+
+
+def stack_heads(pair, first, scale):
+    wide = pair.astype(F32) * scale
+    zero = jnp.zeros_like(wide)
+    return jnp.concatenate(
+        [jnp.where(first, wide, zero), jnp.where(first, zero, wide)], axis=0
+    ).astype(BF)
+
+
+def unstack_heads(both, first):
+    rows = both.shape[0] // 2
+    return jnp.where(first, both[:rows], both[rows:])
+
+
+def norm_parts(rows):
+    centred = rows - jnp.mean(rows, axis=1, keepdims=True)
+    spread = jnp.mean(centred * centred, axis=1, keepdims=True)
+    inverse = lax.rsqrt(spread + 1e-05)
+    return centred * inverse, inverse
+
+
+def norm_pull(grad, hat, inverse, gain):
+    scaled = grad * gain
+    inner = scaled - jnp.mean(scaled, axis=1, keepdims=True)
+    inner = inner - hat * jnp.mean(scaled * hat, axis=1, keepdims=True)
+    return (
+        inverse * inner,
+        jnp.sum(grad * hat, axis=0, keepdims=True),
+        jnp.sum(grad, axis=0, keepdims=True),
+    )
+
+
+def deal_blocks(routes_ref, memory_ref, out_ref):
+    out_ref[...] = jnp.zeros_like(out_ref)
+    blocks = memory_ref.shape[0] // BLK
+    width = memory_ref.shape[1]
+    for b in range(blocks):
+        group = routes_ref[0, b]
+        rank = jnp.int32(0)
+        for earlier in range(b):
+            rank = rank + (routes_ref[0, earlier] == group).astype(jnp.int32)
+        row = pl.multiple_of(rank * BLK, BLK)
+        lane = pl.multiple_of(rank * (width // 2), LANES)
+        out_ref[group, pl.ds(row, BLK), :] = memory_ref[b * BLK : (b + 1) * BLK, :]
+        out_ref[group, 2 * BLK : 2 * BLK + 16, pl.ds(lane, width // 2)] = jnp.ones(
+            (16, width // 2), BF
+        )
+
+
+def self_forward(tok, w_in, w_out, w_q, gain, shift, joined, r1, qc, turned):
+    width = tok.shape[1]
+    rows = tok.shape[0]
+    joined[...] = dot_nn(tok[...], w_in[...]).astype(BF)
+    first = head_masks(rows)
+    mixed = []
+    for j in range(PAIRS):
+        at = j * LANES
+        q2 = stack_heads(joined[:, at : at + LANES], first, FACTOR)
+        key = joined[:, width + at : width + at + LANES]
+        value = joined[:, 2 * width + at : 2 * width + at + LANES]
+        scores = dot_nt(q2, key)
+        power = jnp.exp(scores - jnp.max(scores, axis=1, keepdims=True))
+        prob = (power / jnp.sum(power, axis=1, keepdims=True)).astype(BF)
+        mixed.append(unstack_heads(dot_nn(prob, value), first).astype(BF))
+    o1 = jnp.concatenate(mixed, axis=1)
+    res = tok[...].astype(F32) + dot_nn(o1, w_out[...])
+    r1[...] = res
+    hat, _ = norm_parts(res)
+    h1 = (hat * gain[...].astype(F32) + shift[...].astype(F32)).astype(BF)
+    qc[...] = dot_nn(h1, w_q[...]).astype(BF)
+    turned[0:width, :] = tok[...].T
+    turned[width : 2 * width, :] = o1.T
+    turned[2 * width : 3 * width, :] = h1.T
+
+
+def cross_forward(qc, parcels, w_kv, o2, kv, sums, s_ref, p_ref, bias_ref):
+    width = qc.shape[1]
+    rows = qc.shape[0]
+    sources = parcels.shape[0]
+    span = 2 * BLK
+    first = head_masks(rows)
+    for k in range(sources):
+        kv[k * span : (k + 1) * span, :] = dot_nn(parcels[k, 0:span, :], w_kv[...]).astype(BF)
+        for c in range(2):
+            flag = parcels[k, span : span + 16, c * (width // 2) : c * (width // 2) + BLK]
+            bias_ref[:, k * span + c * BLK : k * span + (c + 1) * BLK] = jnp.where(
+                flag[0:8].astype(F32) > 0.5, 0.0, -1e30
+            )
+    lane = lax.broadcasted_iota(jnp.int32, (2 * rows, LANES), 1)
+    sums[...] = jnp.zeros_like(sums)
+
+    def one_pair(j, carry):
+        at = pl.multiple_of(j * LANES, LANES)
+        q2 = stack_heads(qc[:, pl.ds(at, LANES)], first, FACTOR)
+        top = None
+        for k in range(sources):
+            key = kv[k * span : (k + 1) * span, pl.ds(at, LANES)]
+            scores = dot_nt(q2, key) + bias_ref[0:1, k * span : (k + 1) * span]
+            s_ref[:, k * span : (k + 1) * span] = scores
+            most = jnp.maximum(scores[:, :LANES], scores[:, LANES:])
+            top = most if top is None else jnp.maximum(top, most)
+        peak = jnp.max(top, axis=1, keepdims=True)
+        total = None
+        for k in range(sources):
+            power = jnp.exp(s_ref[:, k * span : (k + 1) * span] - peak)
+            p_ref[:, k * span : (k + 1) * span] = power.astype(BF)
+            part = power[:, :LANES] + power[:, LANES:]
+            total = part if total is None else total + part
+        total = jnp.sum(total, axis=1, keepdims=True)
+        value = kv[:, pl.ds(pl.multiple_of(width + j * LANES, LANES), LANES)]
+        both = dot_nn(p_ref[...], value) / total
+        o2[:, pl.ds(at, LANES)] = unstack_heads(both, first).astype(BF)
+        sums[...] = jnp.where(lane == j, peak + jnp.log(total), sums[...])
+        return carry
+
+    lax.fori_loop(0, PAIRS, one_pair, 0)
+
+
+def feed_forward(
+    rep_ref, o2, tok_h1, sums, w_co, w_up, w_down, b_up, b_down, vec, cot,
+    layer_out, dr2, do2, both_sums, turned_sums, small, small_up,
+    full_rows, xg0, xg1, xg2, xg3, xa0, xa1, xa2, xa3,
+    slope, acts, dus,
+):
+    width = o2.shape[1]
+    rows = o2.shape[0]
+    hidden = w_up.shape[1]
+    quarter = hidden // 4
+    rep = rep_ref[0]
+    gain2, shift2, gain3, shift3 = (vec[i : i + 1, :].astype(F32) for i in range(4))
+    res2 = tok_h1[...].astype(F32) + dot_nn(o2[...], w_co[...])
+    hat2, inv2 = norm_parts(res2)
+    h2 = (hat2 * gain2 + shift2).astype(BF)
+    full_rows[0:width, :] = h2.T
+    full_rows[width : 2 * width, :] = o2[...].T
+    total = None
+    for c in range(4):
+        cols = slice(c * quarter, (c + 1) * quarter)
+        u = dot_nn(h2, w_up[:, cols]) + b_up[:, cols].astype(F32)
+        cdf = 0.5 + 0.5 * lax.erf(u * 0.7071067811865476)
+        act = (u * cdf).astype(BF)
+        slope[:, cols] = cdf + u * (jnp.exp(u * u * -0.5) * 0.3989422804014327)
+        acts[cols, :] = act.T
+        part = dot_nn(act, w_down[cols, :])
+        total = part if total is None else total + part
+    res3 = h2.astype(F32) + total + b_down[...].astype(F32)
+    hat3, inv3 = norm_parts(res3)
+    layer_out[...] = (hat3 * gain3 + shift3).astype(BF)
+    dr3, d_gain3, d_shift3 = norm_pull(cot[...].astype(F32), hat3, inv3, gain3)
+    dy3 = dr3.astype(BF)
+    small[0:1, :] = jnp.sum(dy3.astype(F32), axis=0, keepdims=True)
+    small[3:4, :] = d_gain3
+    small[4:5, :] = d_shift3
+    back = None
+    for c in range(4):
+        cols = slice(c * quarter, (c + 1) * quarter)
+        du = (dot_nt(dy3, w_down[cols, :]) * slope[:, cols]).astype(BF)
+        small_up[:, cols] = jnp.sum(du.astype(F32), axis=0, keepdims=True)
+        dus[c] = du
+        part = dot_nt(du, w_up[:, cols])
+        back = part if back is None else back + part
+    grad2, d_gain2, d_shift2 = norm_pull(dr3 + back, hat2, inv2, gain2)
+    small[1:2, :] = d_gain2
+    small[2:3, :] = d_shift2
+    small[5:8, :] = jnp.zeros((3, width), F32)
+    dr2[...] = grad2
+    dy2 = grad2.astype(BF)
+    grad_mixed = dot_nt(dy2, w_co[...]).astype(BF)
+    do2[...] = grad_mixed
+    lane = lax.broadcasted_iota(jnp.int32, (2 * rows, LANES), 1)
+    first = head_masks(rows)
+    packed = sums[...]
+    for j in range(PAIRS):
+        at = slice(j * LANES, (j + 1) * LANES)
+        prod = grad_mixed[:, at].astype(F32) * o2[:, at].astype(F32)
+        zero = jnp.zeros_like(prod)
+        two = jnp.concatenate([jnp.where(first, prod, zero), jnp.where(first, zero, prod)], axis=0)
+        packed = jnp.where(lane == 8 + j, jnp.sum(two, axis=1, keepdims=True), packed)
+    both_sums[...] = packed
+    turned_sums[...] = packed.T[0:16, :]
+    share = width // 4
+    dy2_of = [dy2[:, i * share : (i + 1) * share] for i in range(4)]
+    acts_rows = width // 8
+    for k, (xg, xa) in enumerate(((xg0, xa0), (xg1, xa1), (xg2, xa2), (xg3, xa3))):
+        peer = rep ^ k
+        xg[:, 0:quarter] = dus[peer]
+        piece = dy2_of[0]
+        for i in range(1, 4):
+            piece = jnp.where(peer == i, dy2_of[i], piece)
+        xg[:, quarter : quarter + share] = piece
+        for s in range(8):
+            row = pl.multiple_of(s * 4 * acts_rows + peer * acts_rows, acts_rows)
+            xa[s * acts_rows : (s + 1) * acts_rows, :] = acts[pl.ds(row, acts_rows), :]
+    full_rows[2 * width : 3 * width, :] = dy3.T
+
+
+def cross_self_backward(
+    rep_ref, qc, do2, kv, parcels, sums, dr2, r1, joined, w_q, w_out, w_in, gain,
+    d_tok, small, yq0, yq1, yq2, yq3, za0, za1, za2, za3,
+    bias_ref, dqc_ref, da_ref, quarters,
+):
+    width = qc.shape[1]
+    rows = qc.shape[0]
+    sources = parcels.shape[0]
+    span = 2 * BLK
+    rep = rep_ref[0]
+    first = head_masks(rows)
+    for k in range(sources):
+        for c in range(2):
+            flag = parcels[k, span : span + 16, c * (width // 2) : c * (width // 2) + BLK]
+            bias_ref[:, k * span + c * BLK : k * span + (c + 1) * BLK] = jnp.where(
+                flag[0:8].astype(F32) > 0.5, 0.0, -1e30
+            )
+    lane = lax.broadcasted_iota(jnp.int32, (2 * rows, LANES), 1)
+
+    def one_pair(j, carry):
+        at = pl.multiple_of(j * LANES, LANES)
+        q2 = stack_heads(qc[:, pl.ds(at, LANES)], first, FACTOR)
+        g2 = stack_heads(do2[:, pl.ds(at, LANES)], first, 1.0)
+        packed = sums[...]
+        log_sum = jnp.sum(jnp.where(lane == j, packed, 0.0), axis=1, keepdims=True)
+        delta = jnp.sum(jnp.where(lane == j + 8, packed, 0.0), axis=1, keepdims=True)
+        total = None
+        for k in range(sources):
+            key = kv[k * span : (k + 1) * span, pl.ds(at, LANES)]
+            value = kv[
+                k * span : (k + 1) * span, pl.ds(pl.multiple_of(width + j * LANES, LANES), LANES)
+            ]
+            scores = dot_nt(q2, key) + bias_ref[0:1, k * span : (k + 1) * span]
+            prob = jnp.exp(scores - log_sum)
+            grad = (prob * (dot_nt(g2, value) - delta)).astype(BF)
+            part = dot_nn(grad, key)
+            total = part if total is None else total + part
+        dqc_ref[:, pl.ds(at, LANES)] = (unstack_heads(total, first) * FACTOR).astype(BF)
+        return carry
+
+    lax.fori_loop(0, PAIRS, one_pair, 0)
+    dqc = dqc_ref[...]
+    grad1 = dr2[...] + dot_nt(dqc, w_q[...])
+    hat1, inv1 = norm_parts(r1[...])
+    dr1, d_gain1, d_shift1 = norm_pull(grad1, hat1, inv1, gain[...].astype(F32))
+    small[0:1, :] = d_gain1
+    small[1:2, :] = d_shift1
+    small[2:8, :] = jnp.zeros((6, width), F32)
+    dy1 = dr1.astype(BF)
+    do1 = dot_nt(dy1, w_out[...]).astype(BF)
+    for j in range(PAIRS):
+        at = slice(j * LANES, (j + 1) * LANES)
+        key_at = slice(width + j * LANES, width + (j + 1) * LANES)
+        value_at = slice(2 * width + j * LANES, 2 * width + (j + 1) * LANES)
+        q2 = stack_heads(joined[:, at], first, FACTOR)
+        g2 = stack_heads(do1[:, at], first, 1.0)
+        key, value = joined[:, key_at], joined[:, value_at]
+        scores = dot_nt(q2, key)
+        power = jnp.exp(scores - jnp.max(scores, axis=1, keepdims=True))
+        prob = power / jnp.sum(power, axis=1, keepdims=True)
+        d_prob = dot_nt(g2, value)
+        d_scores = (prob * (d_prob - jnp.sum(d_prob * prob, axis=1, keepdims=True))).astype(BF)
+        da_ref[:, at] = (unstack_heads(dot_nn(d_scores, key), first) * FACTOR).astype(BF)
+        da_ref[:, key_at] = product_left(d_scores, q2).astype(BF)
+        da_ref[:, value_at] = product_left(prob.astype(BF), g2).astype(BF)
+    d_tok[...] = dr1 + dot_nt(da_ref[...], w_in[...])
+    third = 3 * width // 4
+    share = width // 4
+    da = da_ref[...]
+    for i in range(4):
+        quarters[i, :, 0:third] = da[:, i * third : (i + 1) * third]
+        quarters[i, :, third : third + share] = dy1[:, i * share : (i + 1) * share]
+        quarters[i, :, width : width + share] = dqc[:, i * share : (i + 1) * share]
+    for k, (yq, za) in enumerate(((yq0, za0), (yq1, za1), (yq2, za2), (yq3, za3))):
+        yq[...] = quarters[rep ^ k, :, width : width + share]
+        za[...] = quarters[rep ^ k, :, 0:width]
+
+
+def owner_backward(where_ref, *refs):
+    groups = 8
+    qc, do2, sums = refs[0:groups], refs[groups : 2 * groups], refs[2 * groups : 3 * groups]
+    kv, dkv, q_ref, g_ref, sum_ref = refs[3 * groups :]
+    rows, width = qc[0].shape
+    first = head_masks(rows)
+    for k in range(groups):
+        sum_ref[k] = sums[k][...]
+        for j in range(PAIRS):
+            at = slice(j * LANES, (j + 1) * LANES)
+            q_ref[k, j] = stack_heads(qc[k][:, at], first, FACTOR)
+            g_ref[k, j] = stack_heads(do2[k][:, at], first, 1.0)
+    blocks = kv.shape[0] // BLK
+
+    def one_block(b, carry):
+        group = where_ref[b]
+        row = pl.multiple_of(b * BLK, BLK)
+
+        for j in range(PAIRS):
+            key_at = slice(j * LANES, (j + 1) * LANES)
+            value_at = slice(width + j * LANES, width + (j + 1) * LANES)
+            key = kv[pl.ds(row, BLK), key_at]
+            value = kv[pl.ds(row, BLK), value_at]
+            q2 = q_ref[group, j]
+            g2 = g_ref[group, j]
+            log_sum = sum_ref[group, j : j + 1, :]
+            delta = sum_ref[group, 8 + j : 9 + j, :]
+            prob = jnp.exp(dot_nt(key, q2) - log_sum)
+            grad = (prob * (dot_nt(value, g2) - delta)).astype(BF)
+            dkv[pl.ds(row, BLK), key_at] = dot_nn(grad, q2).astype(BF)
+            dkv[pl.ds(row, BLK), value_at] = dot_nn(prob.astype(BF), g2).astype(BF)
+        return carry
+
+    lax.fori_loop(0, blocks, one_block, 0)
+
+
+def weight_blocks(plan, y_ref, *refs):
+    send, keep, left_all, right_all = refs[-4:]
+    arrays = refs[:-4]
+    y = y_ref[0]
+    tall = send.shape[1]
+    width = left_all.shape[0]
+    for lefts, row, rights, col, cols, to in plan:
+        for k, (a, g) in enumerate(zip(lefts, rights)):
+            rows = arrays[g].shape[0]
+            left_all[:, k * rows : (k + 1) * rows] = arrays[a][row : row + width, :]
+            right_all[k * rows : (k + 1) * rows, 0:cols] = arrays[g][:, col : col + cols]
+        right = right_all[:, 0:cols]
+        for z in range(4):
+            for out, bit in ((send, 1 - y), (keep, y)):
+                at = pl.multiple_of((2 * z + bit) * tall, 16)
+                out[z, :, to : to + cols] = dot_nn(left_all[pl.ds(at, tall), :], right).astype(BF)
+
+
+def fast_on_device(
+    queries, memory, routes, w_self, w_self_out, w_cross_q, w_cross_kv, w_cross_out, w_up, b_up,
+    w_down, b_down, gain_one, shift_one, gain_two, shift_two, gain_three, shift_three, cotangent,
+):
+    streams, reps = lax.axis_size("stream"), lax.axis_size("rep")
+    me, rep = lax.axis_index("stream"), lax.axis_index("rep")
+    width = w_self_out.shape[0]
+    hidden = w_up.shape[1]
+    tokens = queries[0]
+    rows = tokens.shape[0]
+    memory_rows = memory[0]
+    y_bit, z_low, z_high = me % 2, (me // 2) % 2, me // 4
+    rep_scalar = rep.reshape(1).astype(jnp.int32)
+    y_scalar = y_bit.reshape(1).astype(jnp.int32)
+
+    def hop(array, stream_flip=0, rep_flip=0):
+        pairs = [
+            (s * reps + r, (s ^ stream_flip) * reps + (r ^ rep_flip))
+            for s in range(streams)
+            for r in range(reps)
+        ]
+        return lax.ppermute(array, AXES, pairs)
+
+    def rep_full(array):
+        far = hop(array, 0, 2)
+        return [array, hop(array, 0, 1), far, hop(far, 0, 1)]
+
+    def rep_each(parts):
+        return [parts[0]] + [hop(parts[k], 0, k) for k in range(1, 4)]
+
+    def stream_full(array):
+        along = [array] + [hop(array, k) for k in (2, 4, 6)]
+        across = [hop(part, 1) for part in along]
+        return [along[k // 2] if k % 2 == 0 else across[k // 2] for k in range(8)]
+
+    def scatter(send, keep):
+        tall, wide = send.shape[1:]
+        got = hop(send, 1)
+        total = (keep.astype(F32) + got.astype(F32)).astype(BF).reshape(2, 2, tall, wide)
+        give = lax.dynamic_index_in_dim(total, 1 - z_low, 1, keepdims=False)
+        mine = lax.dynamic_index_in_dim(total, z_low, 1, keepdims=False)
+        got = hop(give, 2)
+        total = (mine.astype(F32) + got.astype(F32)).astype(BF)
+        give = lax.dynamic_index_in_dim(total, 1 - z_high, 0, keepdims=False)
+        mine = lax.dynamic_index_in_dim(total, z_high, 0, keepdims=False)
+        got = hop(give, 4)
+        return (mine.astype(F32) + got.astype(F32)).astype(BF)
+
+    def gather_quarters(piece):
+        pieces = jnp.stack(rep_full(piece))
+        order = jnp.arange(4, dtype=jnp.int32) ^ rep
+        return jnp.take(pieces, order, axis=0).astype(F32)
+
+    (parcels_out,) = local_kernel(
+        deal_blocks,
+        [like((streams, 2 * BLK + 16, width), BF)],
+        scalars=[routes],
+        arrays=[memory_rows],
+    )
+    parcels = lax.all_to_all(parcels_out, "stream", split_axis=0, concat_axis=0, tiled=True)
+
+    row_of = lambda v: v.reshape(1, -1)
+    joined, r1, qc, turned1 = local_kernel(
+        self_forward,
+        [
+            like((rows, 3 * width), BF),
+            like((rows, width), F32),
+            like((rows, width), BF),
+            like((3 * width, rows), BF),
+        ],
+        arrays=[tokens, w_self, w_self_out, w_cross_q, row_of(gain_one), row_of(shift_one)],
+        flops=2 * rows * width * width * 5,
+    )
+    early = rep_full(turned1)
+    h1 = turned1[2 * width :, :].T
+    kv_own = matmul(memory_rows, w_cross_kv).astype(BF)
+
+    keys = streams * 2 * BLK
+    o2, kv, sums = local_kernel(
+        cross_forward,
+        [like((rows, width), BF), like((keys, 2 * width), BF), like((2 * rows, LANES), F32)],
+        arrays=[qc, parcels, w_cross_kv],
+        scratch=[
+            pltpu.VMEM((2 * rows, keys), F32),
+            pltpu.VMEM((2 * rows, keys), BF),
+            pltpu.VMEM((8, keys), F32),
+        ],
+        flops=2 * keys * width * width * 2,
+    )
+    qc_all = stream_full(lax.optimization_barrier((qc, parcels))[0])
+
+    vec = jnp.concatenate([row_of(v) for v in (gain_two, shift_two, gain_three, shift_three)])
+    share = width // 4
+    results = local_kernel(
+        feed_forward,
+        [
+            like((rows, width), BF),
+            like((rows, width), F32),
+            like((rows, width), BF),
+            like((2 * rows, LANES), F32),
+            like((16, 2 * rows), F32),
+            like((8, width), F32),
+            like((1, hidden), F32),
+            like((3 * width, rows), BF),
+        ]
+        + [like((rows, hidden // 4 + share), BF)] * 4
+        + [like((hidden // 4, rows), BF)] * 4,
+        scalars=[rep_scalar],
+        arrays=[
+            o2, h1, sums, w_cross_out, w_up, w_down, row_of(b_up), row_of(b_down), vec,
+            cotangent[0],
+        ],
+        scratch=[
+            pltpu.VMEM((rows, hidden), F32),
+            pltpu.VMEM((hidden, rows), BF),
+            pltpu.VMEM((4, rows, hidden // 4), BF),
+        ],
+        flops=2 * rows * width * (4 * hidden + 2 * width),
+    )
+    layer_out, dr2, do2, sums2, turned_sums, small_ff, small_up, full_rows = results[:8]
+    xg, xa = results[8:12], results[12:16]
+    do2_all = stream_full(do2)
+    sums_all = stream_full(turned_sums)
+    full_all = rep_full(full_rows)
+    xg_all = rep_each(xg)
+    xa_all = rep_each(xa)
+
+    def blocks_of(plan, arrays, wide):
+        return local_kernel(
+            functools.partial(weight_blocks, plan),
+            [like((4, width // streams, wide), BF)] * 2,
+            scalars=[y_scalar],
+            arrays=arrays,
+            scratch=[pltpu.VMEM((width, 4 * rows), BF), pltpu.VMEM((4 * rows, width), BF)],
+            flops=2 * 4 * rows * width * wide,
+        )
+
+    dy3_all = [part[2 * width :, :].T for part in full_all]
+    ff_send, ff_keep = blocks_of(
+        [
+            ((0, 1, 2, 3), 0, (8, 9, 10, 11), 0, hidden // 4, 0),
+            ((4, 5, 6, 7), 0, (12, 13, 14, 15), 0, width, hidden // 4),
+        ],
+        full_all + xa_all + xg_all + dy3_all,
+        hidden // 4 + width,
+    )
+    ff_piece = scatter(ff_send, ff_keep)
+
+    d_tokens, small_self, *exports = local_kernel(
+        cross_self_backward,
+        [like((rows, width), F32), like((8, width), F32)]
+        + [like((rows, share), BF)] * 4
+        + [like((rows, width), BF)] * 4,
+        scalars=[rep_scalar],
+        arrays=[
+            qc, do2, kv, parcels, sums2, dr2, r1, joined, w_cross_q, w_self_out, w_self,
+            row_of(gain_one),
+        ],
+        scratch=[
+            pltpu.VMEM((8, keys), F32),
+            pltpu.VMEM((rows, width), BF),
+            pltpu.VMEM((rows, 3 * width), BF),
+            pltpu.VMEM((4, rows, width + share), BF),
+        ],
+        flops=2 * rows * width * (5 * width + 6 * keys),
+    )
+    dqc_all = rep_each(exports[:4])
+    da_all = rep_each(exports[4:])
+
+    where = (routes[0] ^ me).astype(jnp.int32)
+    (dkv,) = local_kernel(
+        owner_backward,
+        [like((memory_rows.shape[0], 2 * width), BF)],
+        scalars=[where],
+        arrays=qc_all + do2_all + sums_all + [kv_own],
+        scratch=[
+            pltpu.VMEM((streams, PAIRS, 2 * rows, LANES), BF),
+            pltpu.VMEM((streams, PAIRS, 2 * rows, LANES), BF),
+            pltpu.VMEM((streams, 16, 2 * rows), F32),
+        ],
+        flops=2 * memory_rows.shape[0] * rows * 8 * width,
+    )
+    d_memory = product_right(dkv, w_cross_kv).astype(BF)
+
+    kv_wide = 2 * width // 4
+    d_kv = product_left(memory_rows, dkv).astype(BF).reshape(width, 4, kv_wide)
+    order = jnp.arange(4, dtype=jnp.int32) ^ rep
+    d_kv = jnp.take(d_kv, order, axis=1).transpose(1, 0, 2)
+    got = hop(jnp.stack([d_kv[1], d_kv[3]]), 0, 1)
+    near = d_kv[0].astype(F32) + got[0].astype(F32)
+    far = (d_kv[2].astype(F32) + got[1].astype(F32)).astype(BF)
+    mine = (near + hop(far, 0, 2).astype(F32)).astype(BF)
+    mine = mine.reshape(4, 2, width // streams, kv_wide)
+    kv_keep = lax.dynamic_index_in_dim(mine, y_bit, 1, keepdims=False)
+    kv_send = lax.dynamic_index_in_dim(mine, 1 - y_bit, 1, keepdims=False)
+    kv_piece = scatter(kv_send, kv_keep)
+
+    rest_send, rest_keep = blocks_of(
+        [
+            ((0, 1, 2, 3), 0, (12, 13, 14, 15), 0, 3 * share, 0),
+            ((0, 1, 2, 3), width, (12, 13, 14, 15), 3 * share, share, 3 * share),
+            ((0, 1, 2, 3), 2 * width, (8, 9, 10, 11), 0, share, 4 * share),
+            ((4, 5, 6, 7), width, (16, 17, 18, 19), hidden // 4, share, 5 * share),
+        ],
+        early + full_all + dqc_all + da_all + xg_all,
+        6 * share,
+    )
+    rest_piece = scatter(rest_send, rest_keep)
+
+    ff_quarters = gather_quarters(ff_piece)
+    kv_quarters = gather_quarters(kv_piece)
+    rest_quarters = gather_quarters(rest_piece)
+
+    def columns(quarters, start, wide):
+        return quarters[:, :, start : start + wide].transpose(1, 0, 2).reshape(-1, 4 * wide)
+
+    small = jnp.concatenate([small_ff[0:5], small_self[0:2], small_up.reshape(4, width)])
+    small = lax.psum(small, AXES)
+    tall = width // streams
+    piece = lambda row: lax.dynamic_slice_in_dim(small[row], me * tall, tall, 0)
+    d_b_up = lax.dynamic_slice_in_dim(
+        small[7:11].reshape(-1), me * (hidden // streams), hidden // streams, 0
+    )
+    return (
+        layer_out[None],
+        d_tokens[None],
+        d_memory[None],
+        columns(rest_quarters, 0, 3 * share),
+        columns(rest_quarters, 3 * share, share),
+        columns(rest_quarters, 4 * share, share),
+        columns(kv_quarters, 0, kv_wide),
+        columns(rest_quarters, 5 * share, share),
+        columns(ff_quarters, 0, hidden // 4),
+        d_b_up,
+        ff_quarters[:, :, hidden // 4 :].reshape(-1, width),
+        piece(0),
+        piece(5),
+        piece(6),
+        piece(1),
+        piece(2),
+        piece(3),
+        piece(4),
+    )
+
+
 def solution(mesh):
     in_specs = (
         P("rep", "stream", None),
@@ -360,6 +979,7 @@
         P("stream"),
         P("stream"),
     )
+    small_slice = (mesh.shape["stream"], mesh.shape["rep"]) == (8, 4)
     return jax.shard_map(
-        on_device, mesh=mesh, in_specs=in_specs, out_specs=out_specs, check_vma=False
-    )
+        fast_on_device if small_slice else on_device, mesh=mesh, in_specs=in_specs, out_specs=out_specs, check_vma=False
+    )

time: 2270 us -> 447 us (0.20)
  blocking collectives: 1450 us -> 38.7 us
  matrix products: 313 us -> 15.7 us
  local copies, waits for them, and re-layouts: 281 us -> 63.4 us
  Pallas kernels: 0 us -> 84.9 us
  waiting for transfers between devices: 101 us -> 159 us
  other arithmetic: 63.6 us -> 15 us
  starting transfers between devices: 18.1 us -> 59.5 us
    unnamed x1 -> x0, blocking collectives: 1440 us -> none
    ppermute x0 -> x59, waiting for transfers between devices: none -> 101 us  [hop(): return lax.ppermute(array, AXES, pairs)]
    dot_general x55 -> x1, matrix products: 106 us -> 5.62 us  [matmul(): return jnp.dot(left, right, preferred_element_type=jnp.float32)]
    dot_general x79 -> x1, matrix products: 103 us -> 4.01 us  [product_right(): lax.dot_general(left, right, (((1,), (1,)), ((), ())), preferred_element_...]
    dot_general x55 -> x1, matrix products: 104 us -> 6.04 us  [product_left(): lax.dot_general(left, right, (((0,), (0,)), ((), ())), preferred_element_...]
    pallas_call x0 -> x8, Pallas kernels: none -> 84.9 us  [local_kernel(): pl.pallas_call(body, out_shape=list(out_shape), in_specs=[pl.BlockSpec(me...]
    ppermute x0 -> x59, starting transfers between devices: none -> 52.1 us  [hop(): return lax.ppermute(array, AXES, pairs)]
    psum x1 -> x0, waiting for transfers between devices: 48.8 us -> none  [on_device(): lax.psum(share_self.astype(jnp.bfloat16), 'rep').astype(jnp.float32)]
  transfers between devices with their start and end apart: 4 -> 60, of which waited for: 2 -> 18; matrix products, arithmetic and copies ran while one was open for 12% -> 16% of each run, Pallas kernels for 0% -> 19%
where the time goes in v1:
time: 447 us; the launch traced here: 438 us
  waiting for transfers between devices  159 us (36%)
  Pallas kernels  84.9 us (19%)
  local copies, waits for them, and re-layouts  63.4 us (14%)
  starting transfers between devices  59.5 us (13%)
  blocking collectives  38.7 us (9%)
  matrix products  15.7 us (4%)
  other arithmetic  15 us (3%)
    ppermute x59, waiting for transfers between devices, hop(): return lax.ppermute(array, AXES, pairs)  101 us
    pallas_call x8, Pallas kernels, local_kernel(): pl.pallas_call(body, out_shape=list(out_shape), in_specs=[pl.BlockSpec(me...  84.9 us
    all_to_all x1, waiting for transfers between devices, fast_on_device(): lax.all_to_all(parcels_out, 'stream', split_axis=0, concat_axis=0, tiled=...  58.5 us
    ppermute x59, starting transfers between devices, hop(): return lax.ppermute(array, AXES, pairs)  52.1 us
    psum x1, blocking collectives, fast_on_device(): small = lax.psum(small, AXES)  38.7 us
    unnamed x130, local copies, waits for them, and re-layouts  20.1 us
  transfers between devices with their start and end apart: 60, of which 18 were waited for; matrix products, arithmetic and copies ran while one was open for 16% of the time, Pallas kernels for 19%

profile of v1, /device:TPU:0, one launch (start us, length us, event | category | flops | bytes accessed | tf_op | source)
XLA Modules:
  0.0 438.5 jit_solution(17838697613154935642)
XLA Ops:
  2.7 2.6 shard_map.323
  5.3 7.4 %all-to-all-start = ((bf16[8,272,768]{2,1,0:T(8,128)(2,1)}), bf16[8,272,768]{2,1,0:T(8,128)(2,1)}, u32[]{:S(2)}, u32[]{:S(2)}) async-start(bf16[8,272,768]{2,1,0:T(8,128)(2,1)} %shard_map.323), calls=%async_computation | async-start | bytes 6684672 | tf_op jit(solution)/shard_map/all_to_all | solution.py:754
  12.9 5.0 %shard_map.322 = (bf16[128,2304]{1,0:T(8,128)(2,1)S(1)}, f32[128,768]{1,0:T(8,128)S(1)}, bf16[128,768]{1,0:T(8,128)(2,1)S(1)}, bf16[2304,128]{1,0:T(8,128)(2,1)S(1)}) custom-call(bf16[128,768]{1,0:T(8,128)(2,1)S(1)} %bitcast.126, bf16[768,2304]{1,0:T(8,128)(2,1)} %w_in.3, bf16[768,768]{1,0:T(8,128)(2,1)} %w_out.3, bf16[768,768]{1,0:T(8,128)(2,1)} %w_q.3, ...), custom_call_target="tpu_custom_call" | custom-call | flops 754974720 | bytes 7867392 | tf_op jit(solution)/shard_map/pallas_call | solution.py:340
  23.6 5.6 %convolution_convert_fusion.refs_24_ = bf16[1024,1536]{1,0:T(8,128)(2,1)} fusion(bf16[768,1536]{1,0:T(8,128)(2,1)} %w_kv.1, bf16[1,1024,768]{2,1,0:T(8,128)(2,1)S(1)} %copy-done.2), kind=kOutput, calls=%fused_computation.4 | convolution fusion | flops 2417491968 | bytes 7077888 | tf_op jit(solution)/shard_map/dot_general | solution.py:16
  29.2 58.5 %all-to-all-done.parcels = bf16[8,272,768]{2,1,0:T(8,128)(2,1)} async-done(((bf16[8,272,768]{2,1,0:T(8,128)(2,1)}), bf16[8,272,768]{2,1,0:T(8,128)(2,1)}, u32[]{:S(2)}, u32[]{:S(2)}) %all-to-all-start) | async-done | bytes 3342368 | tf_op jit(solution)/shard_map/all_to_all | solution.py:754
  87.8 17.0 %shard_map.324 = (bf16[128,768]{1,0:T(8,128)(2,1)S(1)}, bf16[2048,1536]{1,0:T(8,128)(2,1)}, f32[256,128]{1,0:T(8,128)S(1)}) custom-call(bf16[128,768]{1,0:T(8,128)(2,1)S(1)} %get-tuple-element.68.qc.refs_0_, bf16[8,272,768]{2,1,0:T(8,128)(2,1)} %all-to-all-done.parcels, bf16[768,1536]{1,0:T(8,128)(2,1)} %w_kv.1), custom_call_target="tpu_custom_call" | custom-call | flops 4831838208 | bytes 12517376 | tf_op jit(solution)/shard_map/pallas_call | solution.py:340
  104.8 11.7 %shard_map.325 = (bf16[128,768]{1,0:T(8,128)(2,1)}, f32[128,768]{1,0:T(8,128)}, bf16[128,768]{1,0:T(8,128)(2,1)S(1)}, f32[256,128]{1,0:T(8,128)S(1)}, f32[16,256...) custom-call(s32[1]{0:T(128)} %bitcast.rep_ref, ...), custom_call_target="tpu_custom_call" | custom-call | flops 2717908992 | bytes 14681600 | tf_op jit(solution)/shard_map/pallas_call | solution.py:340
  123.8 2.3 collective-permute-start.19
  131.4 2.3 collective-permute-start.5
  136.8 21.8 %shard_map.326 = (f32[128,768]{1,0:T(8,128)}, f32[8,768]{1,0:T(8,128)S(1)}, bf16[128,192]{1,0:T(8,128)(2,1)S(1)}, bf16[128,192]{1,0:T(8,128)(2,1)S(1)}, bf16[128...) custom-call(s32[1]{0:T(128)} %bitcast.rep_ref, ...), custom_call_target="tpu_custom_call" | custom-call | flops 3170893824 | bytes 18834944 | tf_op jit(solution)/shard_map/pallas_call | solution.py:340
  169.8 38.7 %psum.7 = f32[11,768]{1,0:T(8,128)} all-reduce(f32[11,768]{1,0:T(8,128)} %pad_maximum_fusion.4), channel_id=1, replica_groups=mesh['stream'=8,'rep'=4] {'stream','rep'}, use_global_device_ids=true, to_apply=%region_0.1 | all-reduce | flops 8448 | bytes 67584 | tf_op jit(solution)/shard_map/psum | solution.py:912
  222.5 6.5 %collective-permute-done.10.refs_12_ = bf16[128,768]{1,0:T(8,128)(2,1)} collective-permute-done((bf16[128,768]{1,0:T(8,128)(2,1)S(1)}, bf16[128,768]{1,0:T(8,128)(2,1)}, u32[]{:S(2)}, u32[]{:S(2)}) %collective-permute-start.10) | collective-permute-done | bytes 196640 | tf_op jit(solution)/shard_map/ppermute | solution.py:716
  233.3 3.8 collective-permute-done.9.refs_11_
  237.1 3.1 collective-permute-done.11.refs_13_
  246.5 15.0 %shard_map.327 = bf16[1024,1536]{1,0:T(8,128)(2,1)} custom-call(s32[8]{0:T(128)S(1)} %copy-done.27, bf16[128,768]{1,0:T(8,128)(2,1)S(1)} %get-tuple-element.68.qc.refs_0_, bf16[128,768]{1,0:T(8,128)(2,1)S(1)} %collective-permute-done.refs_1_, bf16[128,768]{1,0:T(8,128)(2,1)S(1)} %collective-permute-done.1.refs_2_, ...), custom_call_target="tpu_custom_call" | custom-call | flops 1610612736 | bytes 9568256 | tf_op jit(solution)/shard_map/pallas_call | solution.py:340
  261.5 6.0 %convolution_convert_fusion.1 = bf16[1536,768]{1,0:T(8,128)(2,1)} fusion(bf16[1024,1536]{1,0:T(8,128)(2,1)} %shard_map.327, bf16[1,1024,768]{2,1,0:T(8,128)(2,1)S(1)} %copy-done.2), kind=kOutput, calls=%fused_computation.5 | convolution fusion | flops 2417098752 | bytes 7077888 | tf_op jit(solution)/shard_map/dot_general | solution.py:20
  267.5 4.5 %copy.76 = bf16[768,4,384]{2,0,1:T(8,128)(2,1)} copy(bf16[768,4,384]{0,2,1:T(8,128)(2,1)} %bitcast.133) | data formatting | bytes 4718592 | tf_op jit(solution)/shard_map/reshape | solution.py:880
  272.1 4.0 gather_fusion.1
  284.8 3.6 collective-permute-done.29.refs_11_
  301.9 4.5 %collective-permute-done.32.refs_15_ = bf16[128,768]{1,0:T(8,128)(2,1)S(1)} collective-permute-done((bf16[128,768]{1,0:T(8,128)(2,1)S(1)}, bf16[128,768]{1,0:T(8,128)(2,1)S(1)}, u32[]{:S(2)}, u32[]{:S(2)}) %collective-permute-start.32) | collective-permute-done | bytes 196640 | tf_op jit(solution)/shard_map/ppermute | solution.py:716
  309.2 6.3 %shard_map.328 = (bf16[4,96,1152]{2,1,0:T(8,128)(2,1)}, bf16[4,96,1152]{2,1,0:T(8,128)(2,1)}) custom-call(s32[1]{0:T(128)} %bitcast.9.y_ref, bf16[2304,128]{1,0:T(8,128)(2,1)} %copy-done, bf16[2304,128]{1,0:T(8,128)(2,1)} %collective-permute-done.21.refs_1_, bf16[2304,128]{1,0:T(8,128)(2,1)} %collective-permute-done.22.refs_2_, ...), custom_call_target="tpu_custom_call" | custom-call | flops 905969664 | bytes 8454144 | tf_op jit(solution)/shard_map/pallas_call | solution.py:340
  319.5 5.6 %shard_map.329 = (bf16[4,96,1536]{2,1,0:T(8,128)(2,1)}, bf16[4,96,1536]{2,1,0:T(8,128)(2,1)}) custom-call(s32[1]{0:T(128)} %bitcast.9.y_ref, bf16[2304,128]{1,0:T(8,128)(2,1)} %get-tuple-element.70.refs_4_.refs_0_, bf16[2304,128]{1,0:T(8,128)(2,1)} %copy.70.refs_5_.refs_1_, bf16[2304,128]{1,0:T(8,128)(2,1)} %copy.71.refs_6_.refs_2_, ...), custom_call_target="tpu_custom_call" | custom-call | flops 1207959552 | bytes 7274496 | tf_op jit(solution)/shard_map/pallas_call | solution.py:340
  328.5 9.8 %collective-permute-done.36 = bf16[4,96,1152]{2,1,0:T(8,128)(2,1)S(1)} collective-permute-done((bf16[4,96,1152]{2,1,0:T(8,128)(2,1)}, bf16[4,96,1152]{2,1,0:T(8,128)(2,1)S(1)}, u32[]{:S(2)}, u32[]{:S(2)}) %collective-permute-start.36) | collective-permute-done | bytes 884768 | tf_op jit(solution)/shard_map/ppermute | solution.py:716
  339.4 3.4 collective-permute-done.43
  345.3 18.2 %collective-permute-done.53 = bf16[4,96,1536]{2,1,0:T(8,128)(2,1)S(1)} collective-permute-done((bf16[4,96,1536]{2,1,0:T(8,128)(2,1)}, bf16[4,96,1536]{2,1,0:T(8,128)(2,1)S(1)}, u32[]{:S(2)}, u32[]{:S(2)}) %collective-permute-start.53) | collective-permute-done | bytes 1179680 | tf_op jit(solution)/shard_map/ppermute | solution.py:716
  364.8 4.9 %collective-permute-done.44 = bf16[4,96,384]{2,1,0:T(8,128)(2,1)S(1)} collective-permute-done((bf16[4,96,384]{2,1,0:T(8,128)(2,1)S(1)}, bf16[4,96,384]{2,1,0:T(8,128)(2,1)S(1)}, u32[]{:S(2)}, u32[]{:S(2)}) %collective-permute-start.44) | collective-permute-done | bytes 294944 | tf_op jit(solution)/shard_map/ppermute | solution.py:716
  370.8 11.3 %collective-permute-done.45 = bf16[2,96,384]{2,1,0:T(8,128)(2,1)S(1)} collective-permute-done((bf16[2,96,384]{2,1,0:T(8,128)(2,1)S(1)}, bf16[2,96,384]{2,1,0:T(8,128)(2,1)S(1)}, u32[]{:S(2)}, u32[]{:S(2)}) %collective-permute-start.45) | collective-permute-done | bytes 147488 | tf_op jit(solution)/shard_map/ppermute | solution.py:716
  385.2 7.8 %collective-permute-done.46 = bf16[96,384]{1,0:T(8,128)(2,1)S(1)} collective-permute-done((bf16[96,384]{1,0:T(8,128)(2,1)S(1)}, bf16[96,384]{1,0:T(8,128)(2,1)S(1)}, u32[]{:S(2)}, u32[]{:S(2)}) %collective-permute-start.46) | collective-permute-done | bytes 73760 | tf_op jit(solution)/shard_map/ppermute | solution.py:716
  394.2 4.0 fusion
  401.9 4.4 %collective-permute-done.40 = bf16[96,1152]{1,0:T(8,128)(2,1)S(1)} collective-permute-done((bf16[96,1152]{1,0:T(8,128)(2,1)S(1)}, bf16[96,1152]{1,0:T(8,128)(2,1)S(1)}, u32[]{:S(2)}, u32[]{:S(2)}) %collective-permute-start.40) | collective-permute-done | bytes 221216 | tf_op jit(solution)/shard_map/ppermute | solution.py:716
  409.6 8.7 %collective-permute-done.55 = bf16[96,1536]{1,0:T(8,128)(2,1)S(1)} collective-permute-done((bf16[96,1536]{1,0:T(8,128)(2,1)S(1)}, bf16[96,1536]{1,0:T(8,128)(2,1)S(1)}, u32[]{:S(2)}, u32[]{:S(2)}) %collective-permute-start.55) | collective-permute-done | bytes 294944 | tf_op jit(solution)/shard_map/ppermute | solution.py:716
  419.8 7.6 %collective-permute-done.57 = bf16[96,1536]{1,0:T(8,128)(2,1)S(1)} collective-permute-done((bf16[96,1536]{1,0:T(8,128)(2,1)S(1)}, bf16[96,1536]{1,0:T(8,128)(2,1)S(1)}, u32[]{:S(2)}, u32[]{:S(2)}) %collective-permute-start.57) | collective-permute-done | bytes 294944 | tf_op jit(solution)/shard_map/ppermute | solution.py:716
  (311 shorter events, 120.4 us)
Async XLA Ops:
  5.3 82.4 %all-to-all-start = ((bf16[8,272,768]{2,1,0:T(8,128)(2,1)}), bf16[8,272,768]{2,1,0:T(8,128)(2,1)}, u32[]{:S(2)}, u32[]{:S(2)}) async-start(bf16[8,272,768]{2,1,0:T(8,128)(2,1)} %shard_map.323), calls=%async_computation | async-start | bytes 6684672 | tf_op jit(solution)/shard_map/all_to_all | solution.py:754
  19.4 107.8 %collective-permute-start.22 = (bf16[2304,128]{1,0:T(8,128)(2,1)S(1)}, bf16[2304,128]{1,0:T(8,128)(2,1)}, u32[]{:S(2)}, u32[]{:S(2)}) collective-permute-start(bf16[2304,128]{1,0:T(8,128)(2,1)S(1)} %get-tuple-element.58.refs_0_), channel_id=1, source_target_pairs={{0,2},{1,3},{2,0},{3,1},{4,6},{5,7},{6,4},{7,5},{8,10},{9,11},{10,... | collective-permute-start | bytes 1769480 | tf_op jit(solution)/shard_map/ppermute | solution.py:716
  127.2 83.5 %collective-permute-start = (bf16[128,768]{1,0:T(8,128)(2,1)S(1)}, bf16[128,768]{1,0:T(8,128)(2,1)S(1)}, u32[]{:S(2)}, u32[]{:S(2)}) collective-permute-start(bf16[128,768]{1,0:T(8,128)(2,1)S(1)} %get-tuple-element.68.qc.refs_0_), channel_id=1, source_target_pairs={{0,4},{1,5},{2,6},{3,7},{4,0},{5,1},{6,2},{7,3},{8,12},{9,13},{10,... | collective-permute-start | bytes 589832 | tf_op jit(solution)/shard_map/ppermute | solution.py:716
  129.3 83.7 %collective-permute-start.1 = (bf16[128,768]{1,0:T(8,128)(2,1)S(1)}, bf16[128,768]{1,0:T(8,128)(2,1)S(1)}, u32[]{:S(2)}, u32[]{:S(2)}) collective-permute-start(bf16[128,768]{1,0:T(8,128)(2,1)S(1)} %get-tuple-element.68.qc.refs_0_), channel_id=1, source_target_pairs={{0,8},{1,9},{2,10},{3,11},{4,12},{5,13},{6,14},{7,15},{8,0},{9,1},... | collective-permute-start | bytes 589832 | tf_op jit(solution)/shard_map/ppermute | solution.py:716
  129.3 84.6 %collective-permute-start.3 = (bf16[128,768]{1,0:T(8,128)(2,1)S(1)}, bf16[128,768]{1,0:T(8,128)(2,1)S(1)}, u32[]{:S(2)}, u32[]{:S(2)}) collective-permute-start(bf16[128,768]{1,0:T(8,128)(2,1)S(1)} %get-tuple-element.68.qc.refs_0_), channel_id=1, source_target_pairs={{0,16},{1,17},{2,18},{3,19},{4,20},{5,21},{6,22},{7,23},{8,24},{9,... | collective-permute-start | bytes 589832 | tf_op jit(solution)/shard_map/ppermute | solution.py:716
  131.4 84.1 %collective-permute-start.5 = (bf16[128,768]{1,0:T(8,128)(2,1)S(1)}, bf16[128,768]{1,0:T(8,128)(2,1)}, u32[]{:S(2)}, u32[]{:S(2)}) collective-permute-start(bf16[128,768]{1,0:T(8,128)(2,1)S(1)} %get-tuple-element.68.qc.refs_0_), channel_id=1, source_target_pairs={{0,24},{1,25},{2,26},{3,27},{4,28},{5,29},{6,30},{7,31},{8,16},{9,... | collective-permute-start | bytes 589832 | tf_op jit(solution)/shard_map/ppermute | solution.py:716
  134.3 32.6 %collective-permute-start.18 = (f32[16,256]{1,0:T(8,128)}, f32[16,256]{1,0:T(8,128)}, u32[]{:S(2)}, u32[]{:S(2)}) collective-permute-start(f32[16,256]{1,0:T(8,128)} %collective-permute-done.17.refs_20_), channel_id=1, source_target_pairs={{0,4},{1,5},{2,6},{3,7},{4,0},{5,1},{6,2},{7,3},{8,12},{9,13},{10,... | collective-permute-start | bytes 49160 | tf_op jit(solution)/shard_map/ppermute | solution.py:716
  166.9 41.6 %collective-permute-start.20 = (f32[16,256]{1,0:T(8,128)}, f32[16,256]{1,0:T(8,128)}, u32[]{:S(2)}, u32[]{:S(2)}) collective-permute-start(f32[16,256]{1,0:T(8,128)} %copy-done.20), channel_id=1, source_target_pairs={{0,4},{1,5},{2,6},{3,7},{4,0},{5,1},{6,2},{7,3},{8,12},{9,13},{10,... | collective-permute-start | bytes 49160 | tf_op jit(solution)/shard_map/ppermute | solution.py:716
  213.0 16.0 %collective-permute-start.10 = (bf16[128,768]{1,0:T(8,128)(2,1)S(1)}, bf16[128,768]{1,0:T(8,128)(2,1)}, u32[]{:S(2)}, u32[]{:S(2)}) collective-permute-start(bf16[128,768]{1,0:T(8,128)(2,1)S(1)} %get-tuple-element.61.do2.refs_8_), channel_id=1, source_target_pairs={{0,16},{1,17},{2,18},{3,19},{4,20},{5,21},{6,22},{7,23},{8,24},{9,... | collective-permute-start | bytes 589832 | tf_op jit(solution)/shard_map/ppermute | solution.py:716
  213.9 15.7 %collective-permute-start.12 = (bf16[128,768]{1,0:T(8,128)(2,1)S(1)}, bf16[128,768]{1,0:T(8,128)(2,1)}, u32[]{:S(2)}, u32[]{:S(2)}) collective-permute-start(bf16[128,768]{1,0:T(8,128)(2,1)S(1)} %get-tuple-element.61.do2.refs_8_), channel_id=1, source_target_pairs={{0,24},{1,25},{2,26},{3,27},{4,28},{5,29},{6,30},{7,31},{8,16},{9,... | collective-permute-start | bytes 589832 | tf_op jit(solution)/shard_map/ppermute | solution.py:716
  215.4 15.6 %collective-permute-start.2 = (bf16[128,768]{1,0:T(8,128)(2,1)S(1)}, bf16[128,768]{1,0:T(8,128)(2,1)}, u32[]{:S(2)}, u32[]{:S(2)}) collective-permute-start(bf16[128,768]{1,0:T(8,128)(2,1)S(1)} %collective-permute-done.1.refs_2_), channel_id=1, source_target_pairs={{0,4},{1,5},{2,6},{3,7},{4,0},{5,1},{6,2},{7,3},{8,12},{9,13},{10,... | collective-permute-start | bytes 589832 | tf_op jit(solution)/shard_map/ppermute | solution.py:716
  232.8 45.6 %collective-permute-start.21 = (bf16[2304,128]{1,0:T(8,128)(2,1)S(1)}, bf16[2304,128]{1,0:T(8,128)(2,1)}, u32[]{:S(2)}, u32[]{:S(2)}) collective-permute-start(bf16[2304,128]{1,0:T(8,128)(2,1)S(1)} %get-tuple-element.58.refs_0_), channel_id=1, source_target_pairs={{0,1},{1,0},{2,3},{3,2},{4,5},{5,4},{6,7},{7,6},{8,9},{9,8},{10,11... | collective-permute-start | bytes 1769480 | tf_op jit(solution)/shard_map/ppermute | solution.py:716
  232.8 47.3 %collective-permute-start.23 = (bf16[2304,128]{1,0:T(8,128)(2,1)}, bf16[2304,128]{1,0:T(8,128)(2,1)}, u32[]{:S(2)}, u32[]{:S(2)}) collective-permute-start(bf16[2304,128]{1,0:T(8,128)(2,1)} %collective-permute-done.22.refs_2_), channel_id=1, source_target_pairs={{0,1},{1,0},{2,3},{3,2},{4,5},{5,4},{6,7},{7,6},{8,9},{9,8},{10,11... | collective-permute-start | bytes 1769480 | tf_op jit(solution)/shard_map/ppermute | solution.py:716
  237.1 53.2 %collective-permute-start.24 = (bf16[2304,128]{0,1:T(8,128)(2,1)}, bf16[2304,128]{0,1:T(8,128)(2,1)}, u32[]{:S(2)}, u32[]{:S(2)}) collective-permute-start(bf16[2304,128]{0,1:T(8,128)(2,1)} %copy.68), channel_id=1, source_target_pairs={{0,1},{1,0},{2,3},{3,2},{4,5},{5,4},{6,7},{7,6},{8,9},{9,8},{10,11... | collective-permute-start | bytes 1769480 | tf_op jit(solution)/shard_map/ppermute | solution.py:716
  240.2 35.9 %collective-permute-start.25 = (bf16[2304,128]{0,1:T(8,128)(2,1)}, bf16[2304,128]{0,1:T(8,128)(2,1)}, u32[]{:S(2)}, u32[]{:S(2)}) collective-permute-start(bf16[2304,128]{0,1:T(8,128)(2,1)} %copy.68), channel_id=1, source_target_pairs={{0,2},{1,3},{2,0},{3,1},{4,6},{5,7},{6,4},{7,5},{8,10},{9,11},{10,... | collective-permute-start | bytes 1769480 | tf_op jit(solution)/shard_map/ppermute | solution.py:716
  242.3 37.9 %collective-permute-start.27 = (bf16[128,192]{1,0:T(8,128)(2,1)}, bf16[128,192]{1,0:T(8,128)(2,1)}, u32[]{:S(2)}, u32[]{:S(2)}) collective-permute-start(bf16[128,192]{1,0:T(8,128)(2,1)} %copy-done.44), channel_id=1, source_target_pairs={{0,1},{1,0},{2,3},{3,2},{4,5},{5,4},{6,7},{7,6},{8,9},{9,8},{10,11... | collective-permute-start | bytes 147464 | tf_op jit(solution)/shard_map/ppermute | solution.py:716
  276.1 17.4 %collective-permute-start.26 = (bf16[2304,128]{0,1:T(8,128)(2,1)}, bf16[2304,128]{0,1:T(8,128)(2,1)}, u32[]{:S(2)}, u32[]{:S(2)}) collective-permute-start(bf16[2304,128]{0,1:T(8,128)(2,1)} %collective-permute-done.25), channel_id=1, source_target_pairs={{0,1},{1,0},{2,3},{3,2},{4,5},{5,4},{6,7},{7,6},{8,9},{9,8},{10,11... | collective-permute-start | bytes 1769480 | tf_op jit(solution)/shard_map/ppermute | solution.py:716
  288.4 18.6 %collective-permute-start.33 = (bf16[128,960]{1,0:T(8,128)(2,1)}, bf16[128,960]{1,0:T(8,128)(2,1)S(1)}, u32[]{:S(2)}, u32[]{:S(2)}) collective-permute-start(bf16[128,960]{1,0:T(8,128)(2,1)} %get-tuple-element.80), channel_id=1, source_target_pairs={{0,1},{1,0},{2,3},{3,2},{4,5},{5,4},{6,7},{7,6},{8,9},{9,8},{10,11... | collective-permute-start | bytes 737288 | tf_op jit(solution)/shard_map/ppermute | solution.py:716
  288.7 19.5 %collective-permute-start.34 = (bf16[128,960]{1,0:T(8,128)(2,1)}, bf16[128,960]{1,0:T(8,128)(2,1)S(1)}, u32[]{:S(2)}, u32[]{:S(2)}) collective-permute-start(bf16[128,960]{1,0:T(8,128)(2,1)} %get-tuple-element.81), channel_id=1, source_target_pairs={{0,2},{1,3},{2,0},{3,1},{4,6},{5,7},{6,4},{7,5},{8,10},{9,11},{10,... | collective-permute-start | bytes 737288 | tf_op jit(solution)/shard_map/ppermute | solution.py:716
  289.9 18.6 %collective-permute-start.35 = (bf16[128,960]{1,0:T(8,128)(2,1)}, bf16[128,960]{1,0:T(8,128)(2,1)S(1)}, u32[]{:S(2)}, u32[]{:S(2)}) collective-permute-start(bf16[128,960]{1,0:T(8,128)(2,1)} %get-tuple-element.82), channel_id=1, source_target_pairs={{0,3},{1,2},{2,1},{3,0},{4,7},{5,6},{6,5},{7,4},{8,11},{9,10},{10,... | collective-permute-start | bytes 737288 | tf_op jit(solution)/shard_map/ppermute | solution.py:716
  290.2 35.8 %collective-permute-start.42 = (bf16[2,768,384]{2,1,0:T(8,128)(2,1)}, bf16[2,768,384]{2,1,0:T(8,128)(2,1)}, u32[]{:S(2)}, u32[]{:S(2)}) collective-permute-start(bf16[2,768,384]{2,1,0:T(8,128)(2,1)} %pad_maximum_fusion), channel_id=1, source_target_pairs={{0,1},{1,0},{2,3},{3,2},{4,5},{5,4},{6,7},{7,6},{8,9},{9,8},{10,11... | collective-permute-start | bytes 3538952 | tf_op jit(solution)/shard_map/ppermute | solution.py:716
  293.6 12.9 %collective-permute-start.32 = (bf16[128,768]{1,0:T(8,128)(2,1)S(1)}, bf16[128,768]{1,0:T(8,128)(2,1)S(1)}, u32[]{:S(2)}, u32[]{:S(2)}) collective-permute-start(bf16[128,768]{1,0:T(8,128)(2,1)S(1)} %copy-done.35), channel_id=1, source_target_pairs={{0,3},{1,2},{2,1},{3,0},{4,7},{5,6},{6,5},{7,4},{8,11},{9,10},{10,... | collective-permute-start | bytes 589832 | tf_op jit(solution)/shard_map/ppermute | solution.py:716
  306.4 13.1 %collective-permute-start.50 = (bf16[768,128]{1,0:T(8,128)(2,1)S(1)}, bf16[768,128]{1,0:T(8,128)(2,1)S(1)}, u32[]{:S(2)}, u32[]{:S(2)}) collective-permute-start(bf16[768,128]{1,0:T(8,128)(2,1)S(1)} %copy-done.33), channel_id=1, source_target_pairs={{0,1},{1,0},{2,3},{3,2},{4,5},{5,4},{6,7},{7,6},{8,9},{9,8},{10,11... | collective-permute-start | bytes 589832 | tf_op jit(solution)/shard_map/ppermute | solution.py:716
  315.5 22.8 %collective-permute-start.36 = (bf16[4,96,1152]{2,1,0:T(8,128)(2,1)}, bf16[4,96,1152]{2,1,0:T(8,128)(2,1)S(1)}, u32[]{:S(2)}, u32[]{:S(2)}) collective-permute-start(bf16[4,96,1152]{2,1,0:T(8,128)(2,1)} %get-tuple-element.84), channel_id=1, source_target_pairs={{0,4},{1,5},{2,6},{3,7},{4,0},{5,1},{6,2},{7,3},{8,12},{9,13},{10,... | collective-permute-start | bytes 2654216 | tf_op jit(solution)/shard_map/ppermute | solution.py:716
  325.2 38.4 %collective-permute-start.53 = (bf16[4,96,1536]{2,1,0:T(8,128)(2,1)}, bf16[4,96,1536]{2,1,0:T(8,128)(2,1)S(1)}, u32[]{:S(2)}, u32[]{:S(2)}) collective-permute-start(bf16[4,96,1536]{2,1,0:T(8,128)(2,1)} %get-tuple-element.90), channel_id=1, source_target_pairs={{0,4},{1,5},{2,6},{3,7},{4,0},{5,1},{6,2},{7,3},{8,12},{9,13},{10,... | collective-permute-start | bytes 3538952 | tf_op jit(solution)/shard_map/ppermute | solution.py:716
  327.3 15.5 %collective-permute-start.43 = (bf16[768,384]{1,0:T(8,128)(2,1)S(1)}, bf16[768,384]{1,0:T(8,128)(2,1)S(1)}, u32[]{:S(2)}, u32[]{:S(2)}) collective-permute-start(bf16[768,384]{1,0:T(8,128)(2,1)S(1)} %fusion.4), channel_id=1, source_target_pairs={{0,2},{1,3},{2,0},{3,1},{4,6},{5,7},{6,4},{7,5},{8,10},{9,11},{10,... | collective-permute-start | bytes 1769480 | tf_op jit(solution)/shard_map/ppermute | solution.py:716
  338.6 32.1 %collective-permute-start.37 = (bf16[2,96,1152]{2,1,0:T(8,128)(2,1)S(1)}, bf16[2,96,1152]{2,1,0:T(8,128)(2,1)S(1)}, u32[]{:S(2)}, u32[]{:S(2)}) collective-permute-start(bf16[2,96,1152]{2,1,0:T(8,128)(2,1)S(1)} %dynamic-slice_bitcast_fusion.1), channel_id=1, source_target_pairs={{0,8},{1,9},{2,10},{3,11},{4,12},{5,13},{6,14},{7,15},{8,0},{9,1},... | collective-permute-start | bytes 1327112 | tf_op jit(solution)/shard_map/ppermute | solution.py:716
  344.1 25.5 %collective-permute-start.44 = (bf16[4,96,384]{2,1,0:T(8,128)(2,1)S(1)}, bf16[4,96,384]{2,1,0:T(8,128)(2,1)S(1)}, u32[]{:S(2)}, u32[]{:S(2)}) collective-permute-start(bf16[4,96,384]{2,1,0:T(8,128)(2,1)S(1)} %dynamic-slice_bitcast_fusion.3), channel_id=1, source_target_pairs={{0,4},{1,5},{2,6},{3,7},{4,0},{5,1},{6,2},{7,3},{8,12},{9,13},{10,... | collective-permute-start | bytes 884744 | tf_op jit(solution)/shard_map/ppermute | solution.py:716
  363.9 36.7 %collective-permute-start.54 = (bf16[2,96,1536]{2,1,0:T(8,128)(2,1)S(1)}, bf16[2,96,1536]{2,1,0:T(8,128)(2,1)}, u32[]{:S(2)}, u32[]{:S(2)}) collective-permute-start(bf16[2,96,1536]{2,1,0:T(8,128)(2,1)S(1)} %dynamic-slice_bitcast_fusion), channel_id=1, source_target_pairs={{0,8},{1,9},{2,10},{3,11},{4,12},{5,13},{6,14},{7,15},{8,0},{9,1},... | collective-permute-start | bytes 1769480 | tf_op jit(solution)/shard_map/ppermute | solution.py:716
  383.6 15.2 %collective-permute-start.38 = (bf16[96,1152]{1,0:T(8,128)(2,1)S(1)}, bf16[96,1152]{1,0:T(8,128)(2,1)S(1)}, u32[]{:S(2)}, u32[]{:S(2)}) collective-permute-start(bf16[96,1152]{1,0:T(8,128)(2,1)S(1)} %dynamic-slice_bitcast_fusion.4), channel_id=1, source_target_pairs={{0,16},{1,17},{2,18},{3,19},{4,20},{5,21},{6,22},{7,23},{8,24},{9,... | collective-permute-start | bytes 663560 | tf_op jit(solution)/shard_map/ppermute | solution.py:716
  401.9 16.4 %collective-permute-start.55 = (bf16[96,1536]{1,0:T(8,128)(2,1)S(1)}, bf16[96,1536]{1,0:T(8,128)(2,1)S(1)}, u32[]{:S(2)}, u32[]{:S(2)}) collective-permute-start(bf16[96,1536]{1,0:T(8,128)(2,1)S(1)} %dynamic-slice_bitcast_fusion.2), channel_id=1, source_target_pairs={{0,16},{1,17},{2,18},{3,19},{4,20},{5,21},{6,22},{7,23},{8,24},{9,... | collective-permute-start | bytes 884744 | tf_op jit(solution)/shard_map/ppermute | solution.py:716
  419.7 13.9 %collective-permute-start.56 = (bf16[96,1536]{1,0:T(8,128)(2,1)S(1)}, bf16[96,1536]{1,0:T(8,128)(2,1)}, u32[]{:S(2)}, u32[]{:S(2)}) collective-permute-start(bf16[96,1536]{1,0:T(8,128)(2,1)S(1)} %fusion.5), channel_id=1, source_target_pairs={{0,1},{1,0},{2,3},{3,2},{4,5},{5,4},{6,7},{7,6},{8,9},{9,8},{10,11... | collective-permute-start | bytes 884744 | tf_op jit(solution)/shard_map/ppermute | solution.py:716
  (93 other events, 811.7 us)

commit v2 on v1

--- a/solution.py
+++ b/solution.py
@@ -334,9 +334,7 @@
     return [pl.BlockSpec(memory_space=pltpu.VMEM)] * count
 
 
-def local_kernel(body, out_shape, scalars=(), arrays=(), scratch=(), flops=0, limit=52):
-    moved = sum(a.size * a.dtype.itemsize for a in arrays)
-    moved += sum(o.size * o.dtype.itemsize for o in out_shape)
+def local_kernel(body, out_shape, scalars=(), arrays=(), scratch=(), cost=2, limit=52):
     return pl.pallas_call(
         body,
         out_shape=list(out_shape),
@@ -344,7 +342,9 @@
         out_specs=whole_in_vmem(len(out_shape)),
         scratch_shapes=list(scratch),
         compiler_params=pltpu.CompilerParams(vmem_limit_bytes=limit * 1024 * 1024),
-        cost_estimate=pl.CostEstimate(flops=flops, bytes_accessed=moved, transcendentals=0),
+        cost_estimate=pl.CostEstimate(
+            flops=int(cost * 1.15e9), bytes_accessed=int(cost * 1e5), transcendentals=0
+        ),
     )(*scalars, *arrays)
 
 
@@ -366,11 +366,9 @@
 
 
 def stack_heads(pair, first, scale):
-    wide = pair.astype(F32) * scale
-    zero = jnp.zeros_like(wide)
-    return jnp.concatenate(
-        [jnp.where(first, wide, zero), jnp.where(first, zero, wide)], axis=0
-    ).astype(BF)
+    one = jnp.where(first, scale, 0.0).astype(BF)
+    two = jnp.where(first, 0.0, scale).astype(BF)
+    return jnp.concatenate([pair * one, pair * two], axis=0)
 
 
 def unstack_heads(both, first):
@@ -413,7 +411,7 @@
         )
 
 
-def self_forward(tok, w_in, w_out, w_q, gain, shift, joined, r1, qc, turned):
+def self_forward(tok, w_in, w_out, w_q, gain, shift, joined, r1, h1_out, qc, turned):
     width = tok.shape[1]
     rows = tok.shape[0]
     joined[...] = dot_nn(tok[...], w_in[...]).astype(BF)
@@ -433,6 +431,7 @@
     r1[...] = res
     hat, _ = norm_parts(res)
     h1 = (hat * gain[...].astype(F32) + shift[...].astype(F32)).astype(BF)
+    h1_out[...] = h1
     qc[...] = dot_nn(h1, w_q[...]).astype(BF)
     turned[0:width, :] = tok[...].T
     turned[width : 2 * width, :] = o1.T
@@ -484,8 +483,7 @@
 
 def feed_forward(
     rep_ref, o2, tok_h1, sums, w_co, w_up, w_down, b_up, b_down, vec, cot,
-    layer_out, dr2, do2, both_sums, turned_sums, small, small_up,
-    full_rows, xg0, xg1, xg2, xg3, xa0, xa1, xa2, xa3,
+    layer_out, dr2, do2, both_sums, small, small_up, parcel0, parcel1, parcel2, parcel3,
     slope, acts, dus,
 ):
     width = o2.shape[1]
@@ -497,8 +495,9 @@
     res2 = tok_h1[...].astype(F32) + dot_nn(o2[...], w_co[...])
     hat2, inv2 = norm_parts(res2)
     h2 = (hat2 * gain2 + shift2).astype(BF)
-    full_rows[0:width, :] = h2.T
-    full_rows[width : 2 * width, :] = o2[...].T
+    for parcel in (parcel1, parcel2):
+        parcel[0:width, :] = h2.T
+        parcel[width : 2 * width, :] = o2[...].T
     total = None
     for c in range(4):
         cols = slice(c * quarter, (c + 1) * quarter)
@@ -522,7 +521,7 @@
         cols = slice(c * quarter, (c + 1) * quarter)
         du = (dot_nt(dy3, w_down[cols, :]) * slope[:, cols]).astype(BF)
         small_up[:, cols] = jnp.sum(du.astype(F32), axis=0, keepdims=True)
-        dus[c] = du
+        dus[cols, :] = du.T
         part = dot_nt(du, w_up[:, cols])
         back = part if back is None else back + part
     grad2, d_gain2, d_shift2 = norm_pull(dr3 + back, hat2, inv2, gain2)
@@ -532,7 +531,7 @@
     dr2[...] = grad2
     dy2 = grad2.astype(BF)
     grad_mixed = dot_nt(dy2, w_co[...]).astype(BF)
-    do2[...] = grad_mixed
+    do2[0:rows, :] = grad_mixed
     lane = lax.broadcasted_iota(jnp.int32, (2 * rows, LANES), 1)
     first = head_masks(rows)
     packed = sums[...]
@@ -543,33 +542,38 @@
         two = jnp.concatenate([jnp.where(first, prod, zero), jnp.where(first, zero, prod)], axis=0)
         packed = jnp.where(lane == 8 + j, jnp.sum(two, axis=1, keepdims=True), packed)
     both_sums[...] = packed
-    turned_sums[...] = packed.T[0:16, :]
+    turned = packed.T[0:16, :]
+    high = turned.astype(BF)
+    rest = turned - high.astype(F32)
+    middle = rest.astype(BF)
+    low = (rest - middle.astype(F32)).astype(BF)
+    do2[rows : rows + 16, :] = jnp.concatenate([high, middle, low], axis=1)
     share = width // 4
-    dy2_of = [dy2[:, i * share : (i + 1) * share] for i in range(4)]
-    acts_rows = width // 8
-    for k, (xg, xa) in enumerate(((xg0, xa0), (xg1, xa1), (xg2, xa2), (xg3, xa3))):
+    dy2_turned = dy2.T
+    dy3_turned = dy3.T
+    strip = quarter // 8
+    for k, parcel in enumerate((parcel0, parcel1, parcel2, parcel3)):
         peer = rep ^ k
-        xg[:, 0:quarter] = dus[peer]
-        piece = dy2_of[0]
+        base = 0
+        if k in (1, 2):
+            parcel[2 * width : 3 * width, :] = dy3_turned
+            base = 3 * width
+        for s in range(8):
+            row = pl.multiple_of(s * 4 * strip + peer * strip, strip)
+            parcel[base + s * strip : base + (s + 1) * strip, :] = acts[pl.ds(row, strip), :]
+        row = pl.multiple_of(peer * quarter, quarter)
+        parcel[base + quarter : base + 2 * quarter, :] = dus[pl.ds(row, quarter), :]
+        piece = dy2_turned[0:share]
         for i in range(1, 4):
-            piece = jnp.where(peer == i, dy2_of[i], piece)
-        xg[:, quarter : quarter + share] = piece
-        for s in range(8):
-            row = pl.multiple_of(s * 4 * acts_rows + peer * acts_rows, acts_rows)
-            xa[s * acts_rows : (s + 1) * acts_rows, :] = acts[pl.ds(row, acts_rows), :]
-    full_rows[2 * width : 3 * width, :] = dy3.T
-
-
-def cross_self_backward(
-    rep_ref, qc, do2, kv, parcels, sums, dr2, r1, joined, w_q, w_out, w_in, gain,
-    d_tok, small, yq0, yq1, yq2, yq3, za0, za1, za2, za3,
-    bias_ref, dqc_ref, da_ref, quarters,
-):
+            piece = jnp.where(peer == i, dy2_turned[i * share : (i + 1) * share], piece)
+        parcel[base + 2 * quarter : base + 2 * quarter + share, :] = piece
+
+
+def cross_backward(qc, do2, kv, parcels, sums, dqc, bias_ref):
     width = qc.shape[1]
     rows = qc.shape[0]
     sources = parcels.shape[0]
     span = 2 * BLK
-    rep = rep_ref[0]
     first = head_masks(rows)
     for k in range(sources):
         for c in range(2):
@@ -582,7 +586,7 @@
     def one_pair(j, carry):
         at = pl.multiple_of(j * LANES, LANES)
         q2 = stack_heads(qc[:, pl.ds(at, LANES)], first, FACTOR)
-        g2 = stack_heads(do2[:, pl.ds(at, LANES)], first, 1.0)
+        g2 = stack_heads(do2[0:rows, pl.ds(at, LANES)], first, 1.0)
         packed = sums[...]
         log_sum = jnp.sum(jnp.where(lane == j, packed, 0.0), axis=1, keepdims=True)
         delta = jnp.sum(jnp.where(lane == j + 8, packed, 0.0), axis=1, keepdims=True)
@@ -597,10 +601,20 @@
             grad = (prob * (dot_nt(g2, value) - delta)).astype(BF)
             part = dot_nn(grad, key)
             total = part if total is None else total + part
-        dqc_ref[:, pl.ds(at, LANES)] = (unstack_heads(total, first) * FACTOR).astype(BF)
+        dqc[:, pl.ds(at, LANES)] = (unstack_heads(total, first) * FACTOR).astype(BF)
         return carry
 
     lax.fori_loop(0, PAIRS, one_pair, 0)
+
+
+def self_backward(
+    rep_ref, dqc_ref, dr2, r1, joined, w_q, w_out, w_in, gain,
+    d_tok, small, out0, out1, out2, out3,
+    da_ref, quarters,
+):
+    rows, width = dqc_ref.shape
+    rep = rep_ref[0]
+    first = head_masks(rows)
     dqc = dqc_ref[...]
     grad1 = dr2[...] + dot_nt(dqc, w_q[...])
     hat1, inv1 = norm_parts(r1[...])
@@ -633,29 +647,30 @@
         quarters[i, :, 0:third] = da[:, i * third : (i + 1) * third]
         quarters[i, :, third : third + share] = dy1[:, i * share : (i + 1) * share]
         quarters[i, :, width : width + share] = dqc[:, i * share : (i + 1) * share]
-    for k, (yq, za) in enumerate(((yq0, za0), (yq1, za1), (yq2, za2), (yq3, za3))):
-        yq[...] = quarters[rep ^ k, :, width : width + share]
-        za[...] = quarters[rep ^ k, :, 0:width]
+    for k, out in enumerate((out0, out1, out2, out3)):
+        out[...] = quarters[rep ^ k]
 
 
 def owner_backward(where_ref, *refs):
     groups = 8
-    qc, do2, sums = refs[0:groups], refs[groups : 2 * groups], refs[2 * groups : 3 * groups]
-    kv, dkv, q_ref, g_ref, sum_ref = refs[3 * groups :]
-    rows, width = qc[0].shape
+    qc_near, qc_far, do_near, do_far, kv, dkv, q_ref, g_ref, sum_ref = refs
+    _, rows, width = qc_near.shape
     first = head_masks(rows)
     for k in range(groups):
-        sum_ref[k] = sums[k][...]
+        query = (qc_far if k % 2 else qc_near)[k // 2]
+        extra = (do_far if k % 2 else do_near)[k // 2]
+        sums = extra[rows : rows + 16, :].astype(F32)
+        third = width // 3
+        sum_ref[k] = sums[:, 0:third] + sums[:, third : 2 * third] + sums[:, 2 * third :]
         for j in range(PAIRS):
             at = slice(j * LANES, (j + 1) * LANES)
-            q_ref[k, j] = stack_heads(qc[k][:, at], first, FACTOR)
-            g_ref[k, j] = stack_heads(do2[k][:, at], first, 1.0)
+            q_ref[k, j] = stack_heads(query[:, at], first, FACTOR)
+            g_ref[k, j] = stack_heads(extra[0:rows, at], first, 1.0)
     blocks = kv.shape[0] // BLK
 
     def one_block(b, carry):
         group = where_ref[b]
         row = pl.multiple_of(b * BLK, BLK)
-
         for j in range(PAIRS):
             key_at = slice(j * LANES, (j + 1) * LANES)
             value_at = slice(width + j * LANES, width + (j + 1) * LANES)
@@ -674,22 +689,126 @@
     lax.fori_loop(0, blocks, one_block, 0)
 
 
-def weight_blocks(plan, y_ref, *refs):
-    send, keep, left_all, right_all = refs[-4:]
-    arrays = refs[:-4]
-    y = y_ref[0]
+def memory_weights(rep_ref, dkv, memory_turned, keep, send):
+    quarter = dkv.shape[1] // 4
+    rep = rep_ref[0]
+    for k in range(4):
+        at = pl.multiple_of((rep ^ k) * quarter, LANES)
+        out = (keep, send)[k % 2]
+        out[k // 2] = dot_nn(memory_turned[...], dkv[:, pl.ds(at, quarter)]).astype(BF)
+
+
+def memory_backward(dkv, w_kv, d_memory):
+    half = dkv.shape[0] // 2
+    for i in range(2):
+        span = slice(i * half, (i + 1) * half)
+        d_memory[span, :] = dot_nt(dkv[span, :], w_kv[...]).astype(BF)
+
+
+def own_keys(memory_ref, w_kv, kv, turned):
+    kv[...] = dot_nn(memory_ref[...], w_kv[...]).astype(BF)
+    turned[...] = memory_ref[...].T
+
+
+def weight_blocks(plan, extra, bits_ref, *refs):
+    outs, (left_all, right_all, product) = refs[-7:-3], refs[-3:]
+    arrays = refs[:-7]
+    width, depth = left_all.shape
+    rows = depth // 4
+    tall = width // 8
+
+    def blocks_of(group):
+        bit = bits_ref[group]
+        for i in range(4):
+            for out, b in ((outs[2 * group], 1 - bit), (outs[2 * group + 1], bit)):
+                if group == 0:
+                    yield out, i, 2 * i + b
+                else:
+                    yield out, i, 4 * (i // 2) + 2 * b + i % 2
+
+    for lefts, rights, turned, cols, group, to in plan:
+        for k, ((a, row), (g, off)) in enumerate(zip(lefts, rights)):
+            span = slice(k * rows, (k + 1) * rows)
+            left_all[:, span] = arrays[a][row : row + width, :]
+            right = arrays[g][off : off + cols, :].T if turned else arrays[g][:, off : off + cols]
+            right_all[span, 0:cols] = right
+        product[:, 0:cols] = dot_nn(left_all[...], right_all[:, 0:cols])
+        for out, i, block in blocks_of(group):
+            at = pl.multiple_of(block * tall, 16)
+            out[i, 0:tall, to : to + cols] = product[pl.ds(at, tall), 0:cols].astype(BF)
+    if extra is not None:
+        for group in range(2):
+            for out, i, block in blocks_of(group):
+                out[i, tall:, :] = jnp.zeros_like(out[i, tall:, :])
+                if group == 0:
+                    out[i, tall:, 0:LANES] = arrays[extra][block].astype(BF)
+
+
+def fold_two(bits_ref, kept0, got0, kept1, got1, give0, mine0, give1, mine1):
+    for bit, kept, got, give, mine in (
+        (bits_ref[1], kept0, got0, give0, mine0),
+        (bits_ref[0], kept1, got1, give1, mine1),
+    ):
+        for i in range(2):
+            for out, at in ((give, 2 * i + 1 - bit), (mine, 2 * i + bit)):
+                out[i] = (kept[at].astype(F32) + got[at].astype(F32)).astype(BF)
+
+
+def fold_high(bits_ref, *refs):
+    (give, mine), arrays = refs[-2:], refs[:-2]
+    bit = bits_ref[2]
+    for g in range(len(arrays) // 2):
+        kept, got = arrays[2 * g], arrays[2 * g + 1]
+        for out, at in ((give, 1 - bit), (mine, bit)):
+            out[g] = (kept[at].astype(F32) + got[at].astype(F32)).astype(BF)
+
+
+def fold_one(bits_ref, kept, got, give, mine):
+    bit = bits_ref[1]
+    for i in range(2):
+        for out, at in ((give, 2 * i + 1 - bit), (mine, 2 * i + bit)):
+            out[i] = (kept[at].astype(F32) + got[at].astype(F32)).astype(BF)
+
+
+def fold_last(kept, got, out):
+    out[...] = (kept[...].astype(F32) + got[...].astype(F32)).astype(BF)
+
+
+def fold_core(kept, got, near, far):
+    near[...] = kept[0].astype(F32) + got[0].astype(F32)
+    far[...] = (kept[1].astype(F32) + got[1].astype(F32)).astype(BF)
+
+
+def fold_rep(bits_ref, near, got, send, keep):
+    y = bits_ref[0]
     tall = send.shape[1]
-    width = left_all.shape[0]
-    for lefts, row, rights, col, cols, to in plan:
-        for k, (a, g) in enumerate(zip(lefts, rights)):
-            rows = arrays[g].shape[0]
-            left_all[:, k * rows : (k + 1) * rows] = arrays[a][row : row + width, :]
-            right_all[k * rows : (k + 1) * rows, 0:cols] = arrays[g][:, col : col + cols]
-        right = right_all[:, 0:cols]
-        for z in range(4):
-            for out, bit in ((send, 1 - y), (keep, y)):
-                at = pl.multiple_of((2 * z + bit) * tall, 16)
-                out[z, :, to : to + cols] = dot_nn(left_all[pl.ds(at, tall), :], right).astype(BF)
+    for z in range(4):
+        for out, bit in ((send, 1 - y), (keep, y)):
+            at = pl.multiple_of((2 * z + bit) * tall, 16)
+            out[z] = (near[pl.ds(at, tall), :] + got[pl.ds(at, tall), :].astype(F32)).astype(BF)
+
+
+def lay_columns(plan, rep_ref, *refs):
+    pieces, outs, held = refs[0:4], refs[4:-1], refs[-1]
+    rep = rep_ref[0]
+    for k in range(4):
+        held[k] = pieces[k][...]
+    for (group, start, cols, how), out in zip(plan, outs):
+        if how == "sum":
+            tall = out.shape[0]
+            total = None
+            for k in range(4):
+                part = pieces[k][group, pieces[k].shape[1] - tall :, start : start + cols].astype(F32)
+                total = part if total is None else total + part
+            out[...] = total
+            continue
+        tall = out.shape[0] if how == "side" else out.shape[0] // 4
+        for q in range(4):
+            part = held[rep ^ q, group, 0:tall, start : start + cols].astype(F32)
+            if how == "side":
+                out[:, q * cols : (q + 1) * cols] = part
+            else:
+                out[q * tall : (q + 1) * tall, :] = part
 
 
 def fast_on_device(
@@ -700,12 +819,25 @@
     me, rep = lax.axis_index("stream"), lax.axis_index("rep")
     width = w_self_out.shape[0]
     hidden = w_up.shape[1]
+    quarter, share, tall = hidden // 4, width // 4, width // streams
     tokens = queries[0]
     rows = tokens.shape[0]
     memory_rows = memory[0]
-    y_bit, z_low, z_high = me % 2, (me // 2) % 2, me // 4
     rep_scalar = rep.reshape(1).astype(jnp.int32)
-    y_scalar = y_bit.reshape(1).astype(jnp.int32)
+    bits = jnp.stack([me % 2, (me // 2) % 2, me // 4]).astype(jnp.int32)
+    row_of = lambda v: v.reshape(1, -1)
+    last = []
+
+    def after(first, *others):
+        return lax.optimization_barrier((first, others))[0]
+
+    def run(body, outs, arrays, done=(), **more):
+        held = last + list(done)
+        if held:
+            arrays = [after(arrays[0], *held)] + list(arrays[1:])
+        results = local_kernel(body, outs, arrays=arrays, **more)
+        last[:] = results[:1]
+        return results
 
     def hop(array, stream_flip=0, rep_flip=0):
         pairs = [
@@ -715,6 +847,13 @@
         ]
         return lax.ppermute(array, AXES, pairs)
 
+    def stream_along(array):
+        return [hop(array, k) for k in (2, 4, 6)]
+
+    def stream_across(array, near):
+        near = jnp.stack([array] + near)
+        return [near, hop(near, 1)]
+
     def rep_full(array):
         far = hop(array, 0, 2)
         return [array, hop(array, 0, 1), far, hop(far, 0, 1)]
@@ -722,211 +861,282 @@
     def rep_each(parts):
         return [parts[0]] + [hop(parts[k], 0, k) for k in range(1, 4)]
 
-    def stream_full(array):
-        along = [array] + [hop(array, k) for k in (2, 4, 6)]
-        across = [hop(part, 1) for part in along]
-        return [along[k // 2] if k % 2 == 0 else across[k // 2] for k in range(8)]
-
-    def scatter(send, keep):
-        tall, wide = send.shape[1:]
-        got = hop(send, 1)
-        total = (keep.astype(F32) + got.astype(F32)).astype(BF).reshape(2, 2, tall, wide)
-        give = lax.dynamic_index_in_dim(total, 1 - z_low, 1, keepdims=False)
-        mine = lax.dynamic_index_in_dim(total, z_low, 1, keepdims=False)
-        got = hop(give, 2)
-        total = (mine.astype(F32) + got.astype(F32)).astype(BF)
-        give = lax.dynamic_index_in_dim(total, 1 - z_high, 0, keepdims=False)
-        mine = lax.dynamic_index_in_dim(total, z_high, 0, keepdims=False)
-        got = hop(give, 4)
-        return (mine.astype(F32) + got.astype(F32)).astype(BF)
-
-    def gather_quarters(piece):
-        pieces = jnp.stack(rep_full(piece))
-        order = jnp.arange(4, dtype=jnp.int32) ^ rep
-        return jnp.take(pieces, order, axis=0).astype(F32)
-
-    (parcels_out,) = local_kernel(
+    (parcels_out,) = run(
         deal_blocks,
         [like((streams, 2 * BLK + 16, width), BF)],
+        [memory_rows],
         scalars=[routes],
-        arrays=[memory_rows],
     )
     parcels = lax.all_to_all(parcels_out, "stream", split_axis=0, concat_axis=0, tiled=True)
-
-    row_of = lambda v: v.reshape(1, -1)
-    joined, r1, qc, turned1 = local_kernel(
+    joined, r1, h1, qc, turned1 = run(
         self_forward,
         [
             like((rows, 3 * width), BF),
             like((rows, width), F32),
             like((rows, width), BF),
+            like((rows, width), BF),
             like((3 * width, rows), BF),
         ],
-        arrays=[tokens, w_self, w_self_out, w_cross_q, row_of(gain_one), row_of(shift_one)],
-        flops=2 * rows * width * width * 5,
+        [tokens, w_self, w_self_out, w_cross_q, row_of(gain_one), row_of(shift_one)],
+        cost=5,
     )
     early = rep_full(turned1)
-    h1 = turned1[2 * width :, :].T
-    kv_own = matmul(memory_rows, w_cross_kv).astype(BF)
-
+    kv_own, memory_turned = run(
+        own_keys,
+        [like((memory_rows.shape[0], 2 * width), BF), like(memory_rows.shape[::-1], BF)],
+        [memory_rows, w_cross_kv],
+        cost=6,
+    )
     keys = streams * 2 * BLK
-    o2, kv, sums = local_kernel(
+    o2, kv, sums = run(
         cross_forward,
         [like((rows, width), BF), like((keys, 2 * width), BF), like((2 * rows, LANES), F32)],
-        arrays=[qc, parcels, w_cross_kv],
+        [qc, parcels, w_cross_kv],
+        done=early,
         scratch=[
             pltpu.VMEM((2 * rows, keys), F32),
             pltpu.VMEM((2 * rows, keys), BF),
             pltpu.VMEM((8, keys), F32),
         ],
-        flops=2 * keys * width * width * 2,
-    )
-    qc_all = stream_full(lax.optimization_barrier((qc, parcels))[0])
+        cost=17,
+    )
+
+    qc_near = stream_along(after(qc, parcels))
+    qc_all = stream_across(qc, qc_near)
 
     vec = jnp.concatenate([row_of(v) for v in (gain_two, shift_two, gain_three, shift_three)])
-    share = width // 4
-    results = local_kernel(
+    each = 2 * quarter + share
+    layer_out, dr2, do2, sums2, small_ff, small_up, *parts = run(
         feed_forward,
         [
             like((rows, width), BF),
             like((rows, width), F32),
-            like((rows, width), BF),
+            like((rows + 16, width), BF),
             like((2 * rows, LANES), F32),
-            like((16, 2 * rows), F32),
             like((8, width), F32),
             like((1, hidden), F32),
-            like((3 * width, rows), BF),
         ]
-        + [like((rows, hidden // 4 + share), BF)] * 4
-        + [like((hidden // 4, rows), BF)] * 4,
-        scalars=[rep_scalar],
-        arrays=[
+        + [like((each + base, rows), BF) for base in (0, 3 * width, 3 * width, 0)],
+        [
             o2, h1, sums, w_cross_out, w_up, w_down, row_of(b_up), row_of(b_down), vec,
             cotangent[0],
         ],
+        done=qc_near,
+        scalars=[rep_scalar],
         scratch=[
             pltpu.VMEM((rows, hidden), F32),
             pltpu.VMEM((hidden, rows), BF),
-            pltpu.VMEM((4, rows, hidden // 4), BF),
+            pltpu.VMEM((hidden, rows), BF),
         ],
-        flops=2 * rows * width * (4 * hidden + 2 * width),
-    )
-    layer_out, dr2, do2, sums2, turned_sums, small_ff, small_up, full_rows = results[:8]
-    xg, xa = results[8:12], results[12:16]
-    do2_all = stream_full(do2)
-    sums_all = stream_full(turned_sums)
-    full_all = rep_full(full_rows)
-    xg_all = rep_each(xg)
-    xa_all = rep_each(xa)
-
-    def blocks_of(plan, arrays, wide):
-        return local_kernel(
-            functools.partial(weight_blocks, plan),
-            [like((4, width // streams, wide), BF)] * 2,
-            scalars=[y_scalar],
-            arrays=arrays,
-            scratch=[pltpu.VMEM((width, 4 * rows), BF), pltpu.VMEM((4 * rows, width), BF)],
-            flops=2 * 4 * rows * width * wide,
-        )
-
-    dy3_all = [part[2 * width :, :].T for part in full_all]
-    ff_send, ff_keep = blocks_of(
-        [
-            ((0, 1, 2, 3), 0, (8, 9, 10, 11), 0, hidden // 4, 0),
-            ((4, 5, 6, 7), 0, (12, 13, 14, 15), 0, width, hidden // 4),
-        ],
-        full_all + xa_all + xg_all + dy3_all,
-        hidden // 4 + width,
-    )
-    ff_piece = scatter(ff_send, ff_keep)
-
-    d_tokens, small_self, *exports = local_kernel(
-        cross_self_backward,
+        cost=12,
+    )
+    far = hop(parts[2], 0, 2)
+    do2_near = stream_along(do2)
+
+    (dqc,) = run(
+        cross_backward,
+        [like((rows, width), BF)],
+        [qc, do2, kv, parcels, sums2],
+        scratch=[pltpu.VMEM((8, keys), F32)],
+        cost=13,
+    )
+    near, other = hop(after(parts[1], dqc), 0, 1), hop(after(parts[3], dqc), 0, 3)
+    do2_all = stream_across(do2, do2_near)
+    d_tokens, small_self, *exports = run(
+        self_backward,
         [like((rows, width), F32), like((8, width), F32)]
-        + [like((rows, share), BF)] * 4
-        + [like((rows, width), BF)] * 4,
+        + [like((rows, width + share), BF)] * 4,
+        [dqc, dr2, r1, joined, w_cross_q, w_self_out, w_self, row_of(gain_one)],
+        done=[qc_all[1]] + do2_near,
         scalars=[rep_scalar],
-        arrays=[
-            qc, do2, kv, parcels, sums2, dr2, r1, joined, w_cross_q, w_self_out, w_self,
-            row_of(gain_one),
-        ],
         scratch=[
-            pltpu.VMEM((8, keys), F32),
-            pltpu.VMEM((rows, width), BF),
             pltpu.VMEM((rows, 3 * width), BF),
             pltpu.VMEM((4, rows, width + share), BF),
         ],
-        flops=2 * rows * width * (5 * width + 6 * keys),
-    )
-    dqc_all = rep_each(exports[:4])
-    da_all = rep_each(exports[4:])
-
-    where = (routes[0] ^ me).astype(jnp.int32)
-    (dkv,) = local_kernel(
+        cost=9,
+    )
+    grads_all = rep_each(exports)
+    far_full = hop(after(far, small_self), 0, 1)
+
+    shared = [parts[1], near, far, far_full, parts[0], other]
+
+    def full_at(row):
+        return tuple((a, row) for a in (0, 1, 2, 3))
+
+    def each_at(row):
+        return ((4, row), (1, 3 * width + row), (2, 3 * width + row), (5, row))
+
+    def blocks_of(plan, arrays, size, wide, extra=None):
+        return run(
+            functools.partial(weight_blocks, plan, extra),
+            [like((4, size, wide), BF)] * 4,
+            arrays,
+            scalars=[bits],
+            scratch=[
+                pltpu.VMEM((width, 4 * rows), BF),
+                pltpu.VMEM((4 * rows, width), BF),
+                pltpu.VMEM((width, width), F32),
+            ],
+            cost=5,
+        )
+
+    def first_hops(blocks):
+        send0, keep0, send1, keep1 = blocks
+        return [keep0, hop(send0, 1), keep1, hop(send1, 2)]
+
+    def second_hops(arrays):
+        give0, mine0, give1, mine1 = run(
+            fold_two,
+            [like((2,) + arrays[0].shape[1:], BF)] * 4,
+            arrays,
+            scalars=[bits],
+        )
+        return [mine0, hop(give0, 2), mine1, hop(give1, 1)]
+
+    def third_hop(arrays):
+        give, mine = run(
+            fold_high,
+            [like((len(arrays) // 2,) + arrays[0].shape[1:], BF)] * 2,
+            arrays,
+            scalars=[bits],
+        )
+        return [mine, hop(give, 4)]
+
+    def last_hops(arrays):
+        (piece,) = run(fold_last, [like(arrays[0].shape, BF)], arrays)
+        return rep_full(piece)
+
+    def gathered(pieces, plan, shapes):
+        return run(
+            functools.partial(lay_columns, plan),
+            [like(shape, F32) for shape in shapes],
+            pieces,
+            scalars=[rep_scalar],
+            scratch=[pltpu.VMEM((4,) + pieces[0].shape, BF)],
+        )
+
+    ff = first_hops(
+        blocks_of(
+            [
+                (full_at(0), each_at(quarter), True, quarter, 0, 0),
+                (each_at(0), full_at(2 * width), True, width, 1, 0),
+            ],
+            shared,
+            tall,
+            width,
+        )
+    )
+
+    (dkv,) = run(
         owner_backward,
         [like((memory_rows.shape[0], 2 * width), BF)],
-        scalars=[where],
-        arrays=qc_all + do2_all + sums_all + [kv_own],
+        qc_all + do2_all + [kv_own],
+        scalars=[(routes[0] ^ me).astype(jnp.int32)],
         scratch=[
             pltpu.VMEM((streams, PAIRS, 2 * rows, LANES), BF),
             pltpu.VMEM((streams, PAIRS, 2 * rows, LANES), BF),
             pltpu.VMEM((streams, 16, 2 * rows), F32),
         ],
-        flops=2 * memory_rows.shape[0] * rows * 8 * width,
-    )
-    d_memory = product_right(dkv, w_cross_kv).astype(BF)
-
+        cost=12,
+    )
+    ff = second_hops(ff)
+    vectors = jnp.concatenate([small_ff[0:5], small_self[0:2]]).reshape(7, streams, tall)
+    vectors = jnp.pad(vectors.transpose(1, 0, 2), ((0, 0), (0, 0), (0, LANES - tall)))
+    vectors = jnp.concatenate(
+        [
+            vectors,
+            small_up.reshape(streams, -1, LANES),
+            jnp.zeros((streams, 9 - hidden // streams // LANES, LANES), F32),
+        ],
+        axis=1,
+    )
+    own = len(shared)
+    early_at = lambda row: tuple((own + k, row) for k in range(4))
+    grads_at = lambda col: tuple((own + 4 + k, col) for k in range(4))
+    rest = first_hops(
+        blocks_of(
+            [
+                (early_at(0), grads_at(0), False, 3 * share, 0, 0),
+                (early_at(width), grads_at(3 * share), False, share, 1, 0),
+                (early_at(2 * width), grads_at(4 * share), False, share, 1, share),
+                (full_at(width), each_at(2 * quarter), True, share, 1, 2 * share),
+            ],
+            shared + early + grads_all + [vectors],
+            tall + 16,
+            3 * share,
+            own + 8,
+        )
+    )
+    ff = third_hop(ff)
     kv_wide = 2 * width // 4
-    d_kv = product_left(memory_rows, dkv).astype(BF).reshape(width, 4, kv_wide)
-    order = jnp.arange(4, dtype=jnp.int32) ^ rep
-    d_kv = jnp.take(d_kv, order, axis=1).transpose(1, 0, 2)
-    got = hop(jnp.stack([d_kv[1], d_kv[3]]), 0, 1)
-    near = d_kv[0].astype(F32) + got[0].astype(F32)
-    far = (d_kv[2].astype(F32) + got[1].astype(F32)).astype(BF)
-    mine = (near + hop(far, 0, 2).astype(F32)).astype(BF)
-    mine = mine.reshape(4, 2, width // streams, kv_wide)
-    kv_keep = lax.dynamic_index_in_dim(mine, y_bit, 1, keepdims=False)
-    kv_send = lax.dynamic_index_in_dim(mine, 1 - y_bit, 1, keepdims=False)
-    kv_piece = scatter(kv_send, kv_keep)
-
-    rest_send, rest_keep = blocks_of(
+    kv_keep, kv_send = run(
+        memory_weights,
+        [like((2, width, kv_wide), BF)] * 2,
+        [dkv, memory_turned],
+        scalars=[rep_scalar],
+        cost=7,
+    )
+    kv_core = hop(kv_send, 0, 1)
+    (d_memory,) = run(
+        memory_backward,
+        [like(memory_rows.shape, BF)],
+        [dkv, w_cross_kv],
+        cost=6,
+    )
+    near_sum, far_sum = run(
+        fold_core,
+        [like((width, kv_wide), F32), like((width, kv_wide), BF)],
+        [kv_keep, kv_core],
+    )
+    kv_far = hop(far_sum, 0, 2)
+    rest = second_hops(rest)
+    ff = last_hops(ff)
+    send, keep = run(
+        fold_rep,
+        [like((4, tall, kv_wide), BF)] * 2,
+        [near_sum, kv_far],
+        scalars=[bits],
+    )
+    kv_part = [keep, hop(send, 1)]
+    rest = third_hop(rest)
+    give, mine = run(
+        fold_one, [like((2, tall, kv_wide), BF)] * 2, kv_part, scalars=[bits]
+    )
+    kv_part = [mine, hop(give, 2)]
+    g_up, g_down = gathered(
+        ff,
+        [(0, 0, quarter, "side"), (1, 0, width, "below")],
+        [(tall, hidden), (hidden // streams, width)],
+    )
+    kv_part = third_hop(kv_part)
+    rest = last_hops(rest)
+    kv_part = last_hops(kv_part)
+    g_self, g_self_out, g_query, g_out, g_vec = gathered(
+        rest,
         [
-            ((0, 1, 2, 3), 0, (12, 13, 14, 15), 0, 3 * share, 0),
-            ((0, 1, 2, 3), width, (12, 13, 14, 15), 3 * share, share, 3 * share),
-            ((0, 1, 2, 3), 2 * width, (8, 9, 10, 11), 0, share, 4 * share),
-            ((4, 5, 6, 7), width, (16, 17, 18, 19), hidden // 4, share, 5 * share),
+            (0, 0, 3 * share, "side"),
+            (1, 0, share, "side"),
+            (1, share, share, "side"),
+            (1, 2 * share, share, "side"),
+            (0, 0, LANES, "sum"),
         ],
-        early + full_all + dqc_all + da_all + xg_all,
-        6 * share,
-    )
-    rest_piece = scatter(rest_send, rest_keep)
-
-    ff_quarters = gather_quarters(ff_piece)
-    kv_quarters = gather_quarters(kv_piece)
-    rest_quarters = gather_quarters(rest_piece)
-
-    def columns(quarters, start, wide):
-        return quarters[:, :, start : start + wide].transpose(1, 0, 2).reshape(-1, 4 * wide)
-
-    small = jnp.concatenate([small_ff[0:5], small_self[0:2], small_up.reshape(4, width)])
-    small = lax.psum(small, AXES)
-    tall = width // streams
-    piece = lambda row: lax.dynamic_slice_in_dim(small[row], me * tall, tall, 0)
-    d_b_up = lax.dynamic_slice_in_dim(
-        small[7:11].reshape(-1), me * (hidden // streams), hidden // streams, 0
-    )
+        [(tall, 3 * width), (tall, width), (tall, width), (tall, width), (16, LANES)],
+    )
+    (g_kv,) = gathered(kv_part, [(0, 0, kv_wide, "side")], [(tall, 2 * width)])
+    piece = lambda row: g_vec[row, 0:tall]
+    d_b_up = g_vec[7 : 7 + hidden // streams // LANES].reshape(-1)
     return (
         layer_out[None],
         d_tokens[None],
         d_memory[None],
-        columns(rest_quarters, 0, 3 * share),
-        columns(rest_quarters, 3 * share, share),
-        columns(rest_quarters, 4 * share, share),
-        columns(kv_quarters, 0, kv_wide),
-        columns(rest_quarters, 5 * share, share),
-        columns(ff_quarters, 0, hidden // 4),
+        g_self,
+        g_self_out,
+        g_query,
+        g_kv,
+        g_out,
+        g_up,
         d_b_up,
-        ff_quarters[:, :, hidden // 4 :].reshape(-1, width),
+        g_down,
         piece(0),
         piece(5),
         piece(6),

time: 447 us -> 286 us (0.64); the launches traced: 438 us -> 285 us
  waiting for transfers between devices: 159 us -> 101 us
  local copies, waits for them, and re-layouts: 63.4 us -> 14 us
  blocking collectives: 38.7 us -> 0 us
  Pallas kernels: 84.9 us -> 120 us
  matrix products: 15.7 us -> 0 us
  starting transfers between devices: 59.5 us -> 46.4 us
  other arithmetic: 15 us -> 3.13 us
    ppermute x59 -> x42, waiting for transfers between devices: 101 us -> 56.7 us  [hop(): return lax.ppermute(array, AXES, pairs)]
    psum x1 -> x0, blocking collectives: 38.7 us -> none  [fast_on_device(): small = lax.psum(small, AXES)]
    pallas_call x8 -> x26, Pallas kernels: 84.9 us -> 120 us  [local_kernel(): pl.pallas_call(body, out_shape=list(out_shape), in_specs=[pl.BlockSpec(me...]
    dot_general x3 -> x0, matrix products: 15.7 us -> none  [the longest x1 6.04 us: product_left(): lax.dot_general(left, right, (((0,), (0,)), ((), ())), preferred_element_...]
    all_to_all x1, waiting for transfers between devices: 58.5 us -> 43.9 us  [fast_on_device(): lax.all_to_all(parcels_out, 'stream', split_axis=0, concat_axis=0, tiled=...]
    ppermute x59 -> x42, starting transfers between devices: 52.1 us -> 39 us  [hop(): return lax.ppermute(array, AXES, pairs)]
    reshape x9 -> x4, local copies, waits for them, and re-layouts: 11.7 us -> 0.68 us  [the longest x1 0.58 us: fast_on_device(): d_b_up = g_vec[7:7 + hidden // streams // LANES].reshape(-1)]
    unnamed x130 -> x72, local copies, waits for them, and re-layouts: 20.1 us -> 12.2 us
  transfers between devices with their start and end apart: 60 -> 43, of which waited for: 18 -> 15; matrix products, arithmetic and copies ran while one was open for 16% -> 2% of each run, Pallas kernels for 19% -> 34%
where the time goes in v2:
time: 286 us; the launch traced here: 285 us
  Pallas kernels  120 us (42%)
  waiting for transfers between devices  101 us (35%)
  starting transfers between devices  46.4 us (16%)
  local copies, waits for them, and re-layouts  14 us (5%)
  other arithmetic  3.13 us (1%)
    pallas_call x26, Pallas kernels, local_kernel(): pl.pallas_call(body, out_shape=list(out_shape), in_specs=[pl.BlockSpec(me...  120 us
    ppermute x42, waiting for transfers between devices, hop(): return lax.ppermute(array, AXES, pairs)  56.7 us
    all_to_all x1, waiting for transfers between devices, fast_on_device(): lax.all_to_all(parcels_out, 'stream', split_axis=0, concat_axis=0, tiled=...  43.9 us
    ppermute x42, starting transfers between devices, hop(): return lax.ppermute(array, AXES, pairs)  39 us
    unnamed x72, local copies, waits for them, and re-layouts  12.2 us
    all_to_all x1, starting transfers between devices, fast_on_device(): lax.all_to_all(parcels_out, 'stream', split_axis=0, concat_axis=0, tiled=...  7.41 us
  transfers between devices with their start and end apart: 43, of which 15 were waited for; matrix products, arithmetic and copies ran while one was open for 2% of the time, Pallas kernels for 34%

profile of v2, /device:TPU:0, one launch (start us, length us, event | category | flops | bytes accessed | tf_op | source)
XLA Modules:
  0.0 285.4 jit_solution(12692049957912895209)
XLA Ops:
  2.7 2.6 shard_map.322
  5.3 7.4 %all-to-all-start = ((bf16[8,272,768]{2,1,0:T(8,128)(2,1)}), bf16[8,272,768]{2,1,0:T(8,128)(2,1)}, u32[]{:S(2)}, u32[]{:S(2)}) async-start(bf16[8,272,768]{2,1,0:T(8,128)(2,1)} %shard_map.322), calls=%async_computation | async-start | bytes 6684672 | tf_op jit(solution)/shard_map/all_to_all | solution.py:870
  12.8 5.7 %shard_map.323 = (bf16[128,2304]{1,0:T(8,128)(2,1)S(1)}, f32[128,768]{1,0:T(8,128)S(1)}, bf16[128,768]{1,0:T(8,128)(2,1)S(1)}, bf16[128,768]{1,0:T(8,128)(2,1)S(1)}, bf16[2304,128]{1,0:T(8,128)(2,1)}) custom-call(bf16[128,768]{1,0:T(8,128)(2,1)S(1)} %bitcast.45, bf16[768,2304]{1,0:T(8,128)(2,1)} %w_in.3, bf16[768,768]{1,0:T(8,128)(2,1)} %w_out.3, ...), custom_call_target="tpu_custom_call" | custom-call | flops 5750000128 | bytes 500000 | tf_op jit(solution)/shard_map/pallas_call | solution.py:338
  21.8 13.3 %collective-permute-done.1.refs_8_ = bf16[2304,128]{1,0:T(8,128)(2,1)S(1)} collective-permute-done((bf16[2304,128]{1,0:T(8,128)(2,1)}, bf16[2304,128]{1,0:T(8,128)(2,1)S(1)}, u32[]{:S(2)}, u32[]{:S(2)}) %collective-permute-start.1) | collective-permute-done | bytes 589856 | tf_op jit(solution)/shard_map/ppermute | solution.py:848
  35.1 6.7 %shard_map.324 = (bf16[1024,1536]{1,0:T(8,128)(2,1)}, bf16[768,1024]{1,0:T(8,128)(2,1)S(1)}) custom-call(bf16[1024,768]{1,0:T(8,128)(2,1)} %bitcast.43, bf16[768,1536]{1,0:T(8,128)(2,1)} %w_kv.5), custom_call_target="tpu_custom_call" | custom-call | flops 6899999744 | bytes 600000 | tf_op jit(solution)/shard_map/pallas_call | solution.py:338
  43.8 43.9 %all-to-all-done.parcels = bf16[8,272,768]{2,1,0:T(8,128)(2,1)} async-done(((bf16[8,272,768]{2,1,0:T(8,128)(2,1)}), bf16[8,272,768]{2,1,0:T(8,128)(2,1)}, u32[]{:S(2)}, u32[]{:S(2)}) %all-to-all-start) | async-done | bytes 3342368 | tf_op jit(solution)/shard_map/all_to_all | solution.py:870
  87.7 2.8 collective-permute-start.4
  92.1 17.0 %shard_map.325 = (bf16[128,768]{1,0:T(8,128)(2,1)S(1)}, bf16[2048,1536]{1,0:T(8,128)(2,1)}, f32[256,128]{1,0:T(8,128)S(1)}) custom-call(bf16[128,768]{1,0:T(8,128)(2,1)S(1)} %get-tuple-element.123.qc, bf16[8,272,768]{2,1,0:T(8,128)(2,1)} %all-to-all-done.parcels, bf16[768,1536]{1,0:T(8,128)(2,1)} %w_kv.5), custom_call_target="tpu_custom_call" | custom-call | flops 19549999104 | bytes 1700000 | tf_op jit(solution)/shard_map/pallas_call | solution.py:338
  109.1 12.1 %shard_map.326 = (bf16[128,768]{1,0:T(8,128)(2,1)}, f32[128,768]{1,0:T(8,128)S(1)}, bf16[144,768]{1,0:T(8,128)(2,1)S(1)}, f32[256,128]{1,0:T(8,128)S(1)}, f32[8,...) custom-call(s32[1]{0:T(128)} %bitcast.rep_ref, ...), custom_call_target="tpu_custom_call" | custom-call | flops 13799999488 | bytes 1200000 | tf_op jit(solution)/shard_map/pallas_call | solution.py:338
  122.0 2.8 collective-permute-start.8
  129.5 13.6 %shard_map.327.dqc_ref = bf16[128,768]{1,0:T(8,128)(2,1)S(1)} custom-call(bf16[128,768]{1,0:T(8,128)(2,1)S(1)} %get-tuple-element.123.qc, bf16[144,768]{1,0:T(8,128)(2,1)S(1)} %get-tuple-element.124.do2, bf16[2048,1536]{1,0:T(8,128)(2,1)} %get-tuple-element.125.kv, bf16[8,272,768]{2,1,0:T(8,128)(2,1)} %all-to-all-done.parcels, ...), custom_call_target="tpu_custom_call" | custom-call | flops 14949999616 | bytes 1300000 | tf_op jit(solution)/shard_map/pallas_call | solution.py:338
  144.0 9.4 %shard_map.328 = (f32[128,768]{1,0:T(8,128)}, f32[8,768]{1,0:T(8,128)S(1)}, bf16[128,960]{1,0:T(8,128)(2,1)S(1)}, bf16[128,960]{1,0:T(8,128)(2,1)S(1)}, bf16[128...) custom-call(s32[1]{0:T(128)} %bitcast.rep_ref, bf16[128,768]{1,0:T(8,128)(2,1)S(1)} %shard_map.327.dqc_ref, ...), custom_call_target="tpu_custom_call" | custom-call | flops 10350000128 | bytes 900000 | tf_op jit(solution)/shard_map/pallas_call | solution.py:338
  154.1 2.2 pad_maximum_fusion.refs_2_
  159.6 6.7 %collective-permute-done.13.refs_5_ = bf16[1728,128]{1,0:T(8,128)(2,1)S(1)} collective-permute-done((bf16[1728,128]{1,0:T(8,128)(2,1)}, bf16[1728,128]{1,0:T(8,128)(2,1)S(1)}, u32[]{:S(2)}, u32[]{:S(2)}) %collective-permute-start.13) | collective-permute-done | bytes 442400 | tf_op jit(solution)/shard_map/ppermute | solution.py:848
  169.2 4.9 %shard_map.329 = (bf16[4,96,768]{2,1,0:T(8,128)(2,1)S(1)}, bf16[4,96,768]{2,1,0:T(8,128)(2,1)}, bf16[4,96,768]{2,1,0:T(8,128)(2,1)}, bf16[4,96,768]{2,1,0:T(8,128)(2,1)}) custom-call(s32[3]{0:T(128)S(1)} %pad_add_fusion.bits_ref, bf16[4032,128]{1,0:T(8,128)(2,1)} %get-tuple-element.148.refs_0_, bf16[4032,128]{1,0:T(8,128)(2,1)} %collective-permute-done.10.refs_1_, ...), custom_call_target="tpu_custom_call" | custom-call | flops 5750000128 | bytes 500000 | tf_op jit(solution)/shard_map/pallas_call | solution.py:338
  174.7 4.4 %collective-permute-done.14.refs_3_ = bf16[4,144,768]{2,1,0:T(8,128)(2,1)} collective-permute-done((bf16[4,144,768]{2,1,0:T(8,128)(2,1)}, bf16[4,144,768]{2,1,0:T(8,128)(2,1)}, u32[]{:S(2)}, u32[]{:S(2)}) %collective-permute-start.14) | collective-permute-done | bytes 884768 | tf_op jit(solution)/shard_map/ppermute | solution.py:848
  180.8 15.2 %shard_map.330.dkv = bf16[1024,1536]{1,0:T(8,128)(2,1)} custom-call(s32[8]{0:T(128)S(1)} %xor_bitcast_fusion.where_ref, bf16[4,128,768]{2,1,0:T(8,128)(2,1)S(1)} %pad_maximum_fusion.1.refs_0_, bf16[4,128,768]{2,1,0:T(8,128)(2,1)S(1)} %collective-permute-done.6.refs_1_, bf16[4,144,768]{2,1,0:T(8,128)(2,1)} %pad_maximum_fusion.refs_2_, ...), custom_call_target="tpu_custom_call" | custom-call | flops 13799999488 | bytes 1200000 | tf_op jit(solution)/shard_map/pallas_call | solution.py:338
  200.8 6.4 %shard_map.332 = (bf16[4,112,576]{2,1,0:T(8,128)(2,1)}, bf16[4,112,576]{2,1,0:T(8,128)(2,1)}, bf16[4,112,576]{2,1,0:T(8,128)(2,1)}, bf16[4,112,576]{2,1,0:T(8,128)(2,1)}) custom-call(s32[3]{0:T(128)S(1)} %pad_add_fusion.bits_ref, bf16[4032,128]{1,0:T(8,128)(2,1)} %get-tuple-element.148.refs_0_, bf16[4032,128]{1,0:T(8,128)(2,1)} %collective-permute-done.10.refs_1_, ...), custom_call_target="tpu_custom_call" | custom-call | flops 5750000128 | bytes 500000 | tf_op jit(solution)/shard_map/pallas_call | solution.py:338
  208.0 6.9 %shard_map.334 = (bf16[2,768,384]{2,1,0:T(8,128)(2,1)S(1)}, bf16[2,768,384]{2,1,0:T(8,128)(2,1)}) custom-call(s32[1]{0:T(128)} %bitcast.rep_ref, bf16[1024,1536]{1,0:T(8,128)(2,1)} %shard_map.330.dkv, bf16[768,1024]{1,0:T(8,128)(2,1)} %copy-done.9), custom_call_target="tpu_custom_call" | custom-call | flops 8049999872 | bytes 700000 | tf_op jit(solution)/shard_map/pallas_call | solution.py:338
  216.9 6.4 %shard_map.335 = bf16[1024,768]{1,0:T(8,128)(2,1)} custom-call(bf16[1024,1536]{1,0:T(8,128)(2,1)} %shard_map.330.dkv, bf16[768,1536]{1,0:T(8,128)(2,1)} %w_kv.5), custom_call_target="tpu_custom_call" | custom-call | flops 6899999744 | bytes 600000 | tf_op jit(solution)/shard_map/pallas_call | solution.py:338
  224.3 1.9 shard_map.336
  227.8 2.4 collective-permute-start.25
  232.9 10.6 %collective-permute-done.25.got = bf16[2,96,768]{2,1,0:T(8,128)(2,1)S(1)} collective-permute-done((bf16[2,96,768]{2,1,0:T(8,128)(2,1)S(1)}, bf16[2,96,768]{2,1,0:T(8,128)(2,1)S(1)}, u32[]{:S(2)}, u32[]{:S(2)}) %collective-permute-start.25) | collective-permute-done | bytes 294944 | tf_op jit(solution)/shard_map/ppermute | solution.py:848
  248.6 3.1 %collective-permute-done.31.refs_2_ = bf16[2,96,768]{2,1,0:T(8,128)(2,1)S(1)} collective-permute-done((bf16[2,96,768]{2,1,0:T(8,128)(2,1)S(1)}, bf16[2,96,768]{2,1,0:T(8,128)(2,1)S(1)}, u32[]{:S(2)}, u32[]{:S(2)}) %collective-permute-start.31) | collective-permute-done | bytes 294944 | tf_op jit(solution)/shard_map/ppermute | solution.py:848
  253.0 1.9 collective-permute-done.28.refs_3_
  255.5 3.1 %collective-permute-start.34 = (bf16[2,112,576]{2,1,0:T(8,128)(2,1)S(1)}, bf16[2,112,576]{2,1,0:T(8,128)(2,1)S(1)}, u32[]{:S(2)}, u32[]{:S(2)}) collective-permute-start(bf16[2,112,576]{2,1,0:T(8,128)(2,1)S(1)} %get-tuple-element.183), channel_id=1, source_target_pairs={{0,16},{1,17},{2,18},{3,19},{4,20},{5,21},{6,22},{7,23},{8,24},{9,... | collective-permute-start | bytes 774152 | tf_op jit(solution)/shard_map/ppermute | solution.py:848
  259.9 1.8 collective-permute-start.33
  263.3 3.0 %collective-permute-done.33.refs_1_ = bf16[2,96,384]{2,1,0:T(8,128)(2,1)S(1)} collective-permute-done((bf16[2,96,384]{2,1,0:T(8,128)(2,1)S(1)}, bf16[2,96,384]{2,1,0:T(8,128)(2,1)S(1)}, u32[]{:S(2)}, u32[]{:S(2)}) %collective-permute-start.33) | collective-permute-done | bytes 147488 | tf_op jit(solution)/shard_map/ppermute | solution.py:848
  266.9 1.9 collective-permute-done.34.got
  270.2 7.0 %collective-permute-done.37.refs_2_ = bf16[2,112,576]{2,1,0:T(8,128)(2,1)S(1)} collective-permute-done((bf16[2,112,576]{2,1,0:T(8,128)(2,1)S(1)}, bf16[2,112,576]{2,1,0:T(8,128)(2,1)S(1)}, u32[]{:S(2)}, u32[]{:S(2)}) %collective-permute-start.37) | collective-permute-done | bytes 258080 | tf_op jit(solution)/shard_map/ppermute | solution.py:848
  277.1 1.8 collective-permute-start.40
  279.2 2.7 collective-permute-done.40.refs_2_
  (177 shorter events, 52.9 us)
Async XLA Ops:
  5.3 82.4 %all-to-all-start = ((bf16[8,272,768]{2,1,0:T(8,128)(2,1)}), bf16[8,272,768]{2,1,0:T(8,128)(2,1)}, u32[]{:S(2)}, u32[]{:S(2)}) async-start(bf16[8,272,768]{2,1,0:T(8,128)(2,1)} %shard_map.322), calls=%async_computation | async-start | bytes 6684672 | tf_op jit(solution)/shard_map/all_to_all | solution.py:870
  20.1 15.0 %collective-permute-start.1 = (bf16[2304,128]{1,0:T(8,128)(2,1)}, bf16[2304,128]{1,0:T(8,128)(2,1)S(1)}, u32[]{:S(2)}, u32[]{:S(2)}) collective-permute-start(bf16[2304,128]{1,0:T(8,128)(2,1)} %get-tuple-element.115.refs_6_), channel_id=1, source_target_pairs={{0,2},{1,3},{2,0},{3,1},{4,6},{5,7},{6,4},{7,5},{8,10},{9,11},{10,... | collective-permute-start | bytes 1769480 | tf_op jit(solution)/shard_map/ppermute | solution.py:848
  21.6 21.4 %collective-permute-start = (bf16[2304,128]{1,0:T(8,128)(2,1)}, bf16[2304,128]{1,0:T(8,128)(2,1)S(1)}, u32[]{:S(2)}, u32[]{:S(2)}) collective-permute-start(bf16[2304,128]{1,0:T(8,128)(2,1)} %get-tuple-element.115.refs_6_), channel_id=1, source_target_pairs={{0,1},{1,0},{2,3},{3,2},{4,5},{5,4},{6,7},{7,6},{8,9},{9,8},{10,11... | collective-permute-start | bytes 1769480 | tf_op jit(solution)/shard_map/ppermute | solution.py:848
  87.7 21.4 %collective-permute-start.3 = (bf16[128,768]{1,0:T(8,128)(2,1)S(1)}, bf16[128,768]{1,0:T(8,128)(2,1)S(1)}, u32[]{:S(2)}, u32[]{:S(2)}) collective-permute-start(bf16[128,768]{1,0:T(8,128)(2,1)S(1)} %get-tuple-element.123.qc), channel_id=1, source_target_pairs={{0,8},{1,9},{2,10},{3,11},{4,12},{5,13},{6,14},{7,15},{8,0},{9,1},... | collective-permute-start | bytes 589832 | tf_op jit(solution)/shard_map/ppermute | solution.py:848
  87.7 21.4 %collective-permute-start.4 = (bf16[128,768]{1,0:T(8,128)(2,1)S(1)}, bf16[128,768]{1,0:T(8,128)(2,1)S(1)}, u32[]{:S(2)}, u32[]{:S(2)}) collective-permute-start(bf16[128,768]{1,0:T(8,128)(2,1)S(1)} %get-tuple-element.123.qc), channel_id=1, source_target_pairs={{0,16},{1,17},{2,18},{3,19},{4,20},{5,21},{6,22},{7,23},{8,24},{9,... | collective-permute-start | bytes 589832 | tf_op jit(solution)/shard_map/ppermute | solution.py:848
  90.6 18.6 %collective-permute-start.5 = (bf16[128,768]{1,0:T(8,128)(2,1)S(1)}, bf16[128,768]{1,0:T(8,128)(2,1)S(1)}, u32[]{:S(2)}, u32[]{:S(2)}) collective-permute-start(bf16[128,768]{1,0:T(8,128)(2,1)S(1)} %get-tuple-element.123.qc), channel_id=1, source_target_pairs={{0,24},{1,25},{2,26},{3,27},{4,28},{5,29},{6,30},{7,31},{8,16},{9,... | collective-permute-start | bytes 589832 | tf_op jit(solution)/shard_map/ppermute | solution.py:848
  122.0 21.2 %collective-permute-start.7 = (bf16[144,768]{1,0:T(8,128)(2,1)S(1)}, bf16[144,768]{1,0:T(8,128)(2,1)S(1)}, u32[]{:S(2)}, u32[]{:S(2)}) collective-permute-start(bf16[144,768]{1,0:T(8,128)(2,1)S(1)} %get-tuple-element.124.do2), channel_id=1, source_target_pairs={{0,8},{1,9},{2,10},{3,11},{4,12},{5,13},{6,14},{7,15},{8,0},{9,1},... | collective-permute-start | bytes 663560 | tf_op jit(solution)/shard_map/ppermute | solution.py:848
  122.0 21.3 %collective-permute-start.8 = (bf16[144,768]{1,0:T(8,128)(2,1)S(1)}, bf16[144,768]{1,0:T(8,128)(2,1)S(1)}, u32[]{:S(2)}, u32[]{:S(2)}) collective-permute-start(bf16[144,768]{1,0:T(8,128)(2,1)S(1)} %get-tuple-element.124.do2), channel_id=1, source_target_pairs={{0,16},{1,17},{2,18},{3,19},{4,20},{5,21},{6,22},{7,23},{8,24},{9,... | collective-permute-start | bytes 663560 | tf_op jit(solution)/shard_map/ppermute | solution.py:848
  124.8 18.5 %collective-permute-start.9 = (bf16[144,768]{1,0:T(8,128)(2,1)S(1)}, bf16[144,768]{1,0:T(8,128)(2,1)S(1)}, u32[]{:S(2)}, u32[]{:S(2)}) collective-permute-start(bf16[144,768]{1,0:T(8,128)(2,1)S(1)} %get-tuple-element.124.do2), channel_id=1, source_target_pairs={{0,24},{1,25},{2,26},{3,27},{4,28},{5,29},{6,30},{7,31},{8,16},{9,... | collective-permute-start | bytes 663560 | tf_op jit(solution)/shard_map/ppermute | solution.py:848
  126.5 16.8 %collective-permute-start.6 = (bf16[4,128,768]{2,1,0:T(8,128)(2,1)S(1)}, bf16[4,128,768]{2,1,0:T(8,128)(2,1)S(1)}, u32[]{:S(2)}, u32[]{:S(2)}) collective-permute-start(bf16[4,128,768]{2,1,0:T(8,128)(2,1)S(1)} %pad_maximum_fusion.1.refs_0_), channel_id=1, source_target_pairs={{0,4},{1,5},{2,6},{3,7},{4,0},{5,1},{6,2},{7,3},{8,12},{9,13},{10,... | collective-permute-start | bytes 2359304 | tf_op jit(solution)/shard_map/ppermute | solution.py:848
  128.0 25.4 %collective-permute-start.11 = (bf16[4032,128]{1,0:T(8,128)(2,1)S(1)}, bf16[4032,128]{1,0:T(8,128)(2,1)}, u32[]{:S(2)}, u32[]{:S(2)}) collective-permute-start(bf16[4032,128]{1,0:T(8,128)(2,1)S(1)} %copy-done.26), channel_id=1, source_target_pairs={{0,2},{1,3},{2,0},{3,1},{4,6},{5,7},{6,4},{7,5},{8,10},{9,11},{10,... | collective-permute-start | bytes 3096584 | tf_op jit(solution)/shard_map/ppermute | solution.py:848
  143.2 23.7 %collective-permute-start.10 = (bf16[4032,128]{1,0:T(8,128)(2,1)}, bf16[4032,128]{1,0:T(8,128)(2,1)}, u32[]{:S(2)}, u32[]{:S(2)}) collective-permute-start(bf16[4032,128]{1,0:T(8,128)(2,1)} %get-tuple-element.148.refs_0_), channel_id=1, source_target_pairs={{0,1},{1,0},{2,3},{3,2},{4,5},{5,4},{6,7},{7,6},{8,9},{9,8},{10,11... | collective-permute-start | bytes 3096584 | tf_op jit(solution)/shard_map/ppermute | solution.py:848
  153.4 14.7 %collective-permute-start.12 = (bf16[4032,128]{1,0:T(8,128)(2,1)}, bf16[4032,128]{1,0:T(8,128)(2,1)}, u32[]{:S(2)}, u32[]{:S(2)}) collective-permute-start(bf16[4032,128]{1,0:T(8,128)(2,1)} %collective-permute-done.11.refs_2_), channel_id=1, source_target_pairs={{0,1},{1,0},{2,3},{3,2},{4,5},{5,4},{6,7},{7,6},{8,9},{9,8},{10,11... | collective-permute-start | bytes 3096584 | tf_op jit(solution)/shard_map/ppermute | solution.py:848
  153.9 12.4 %collective-permute-start.13 = (bf16[1728,128]{1,0:T(8,128)(2,1)}, bf16[1728,128]{1,0:T(8,128)(2,1)S(1)}, u32[]{:S(2)}, u32[]{:S(2)}) collective-permute-start(bf16[1728,128]{1,0:T(8,128)(2,1)} %get-tuple-element.139), channel_id=1, source_target_pairs={{0,3},{1,2},{2,1},{3,0},{4,7},{5,6},{6,5},{7,4},{8,11},{9,10},{10,... | collective-permute-start | bytes 1327112 | tf_op jit(solution)/shard_map/ppermute | solution.py:848
  156.3 22.8 %collective-permute-start.14 = (bf16[4,144,768]{2,1,0:T(8,128)(2,1)}, bf16[4,144,768]{2,1,0:T(8,128)(2,1)}, u32[]{:S(2)}, u32[]{:S(2)}) collective-permute-start(bf16[4,144,768]{2,1,0:T(8,128)(2,1)} %pad_maximum_fusion.refs_2_), channel_id=1, source_target_pairs={{0,4},{1,5},{2,6},{3,7},{4,0},{5,1},{6,2},{7,3},{8,12},{9,13},{10,... | collective-permute-start | bytes 2654216 | tf_op jit(solution)/shard_map/ppermute | solution.py:848
  159.5 41.3 %collective-permute-start.17 = (bf16[128,960]{1,0:T(8,128)(2,1)S(1)}, bf16[128,960]{1,0:T(8,128)(2,1)S(1)}, u32[]{:S(2)}, u32[]{:S(2)}) collective-permute-start(bf16[128,960]{1,0:T(8,128)(2,1)S(1)} %get-tuple-element.150), channel_id=1, source_target_pairs={{0,1},{1,0},{2,3},{3,2},{4,5},{5,4},{6,7},{7,6},{8,9},{9,8},{10,11... | collective-permute-start | bytes 737288 | tf_op jit(solution)/shard_map/ppermute | solution.py:848
  166.3 34.5 %collective-permute-start.18 = (bf16[128,960]{1,0:T(8,128)(2,1)S(1)}, bf16[128,960]{1,0:T(8,128)(2,1)S(1)}, u32[]{:S(2)}, u32[]{:S(2)}) collective-permute-start(bf16[128,960]{1,0:T(8,128)(2,1)S(1)} %get-tuple-element.151), channel_id=1, source_target_pairs={{0,2},{1,3},{2,0},{3,1},{4,6},{5,7},{6,4},{7,5},{8,10},{9,11},{10,... | collective-permute-start | bytes 737288 | tf_op jit(solution)/shard_map/ppermute | solution.py:848
  166.8 34.0 %collective-permute-start.19 = (bf16[128,960]{1,0:T(8,128)(2,1)S(1)}, bf16[128,960]{1,0:T(8,128)(2,1)S(1)}, u32[]{:S(2)}, u32[]{:S(2)}) collective-permute-start(bf16[128,960]{1,0:T(8,128)(2,1)S(1)} %get-tuple-element.152), channel_id=1, source_target_pairs={{0,3},{1,2},{2,1},{3,0},{4,7},{5,6},{6,5},{7,4},{8,11},{9,10},{10,... | collective-permute-start | bytes 737288 | tf_op jit(solution)/shard_map/ppermute | solution.py:848
  174.1 21.9 %collective-permute-start.15 = (bf16[4,96,768]{2,1,0:T(8,128)(2,1)S(1)}, bf16[4,96,768]{2,1,0:T(8,128)(2,1)S(1)}, u32[]{:S(2)}, u32[]{:S(2)}) collective-permute-start(bf16[4,96,768]{2,1,0:T(8,128)(2,1)S(1)} %get-tuple-element.140), channel_id=1, source_target_pairs={{0,4},{1,5},{2,6},{3,7},{4,0},{5,1},{6,2},{7,3},{8,12},{9,13},{10,... | collective-permute-start | bytes 1769480 | tf_op jit(solution)/shard_map/ppermute | solution.py:848
  179.0 16.9 %collective-permute-start.16 = (bf16[4,96,768]{2,1,0:T(8,128)(2,1)}, bf16[4,96,768]{2,1,0:T(8,128)(2,1)S(1)}, u32[]{:S(2)}, u32[]{:S(2)}) collective-permute-start(bf16[4,96,768]{2,1,0:T(8,128)(2,1)} %get-tuple-element.145), channel_id=1, source_target_pairs={{0,8},{1,9},{2,10},{3,11},{4,12},{5,13},{6,14},{7,15},{8,0},{9,1},... | collective-permute-start | bytes 1769480 | tf_op jit(solution)/shard_map/ppermute | solution.py:848
  198.7 8.5 %collective-permute-start.20 = (bf16[2,96,768]{2,1,0:T(8,128)(2,1)S(1)}, bf16[2,96,768]{2,1,0:T(8,128)(2,1)S(1)}, u32[]{:S(2)}, u32[]{:S(2)}) collective-permute-start(bf16[2,96,768]{2,1,0:T(8,128)(2,1)S(1)} %get-tuple-element.147), channel_id=1, source_target_pairs={{0,8},{1,9},{2,10},{3,11},{4,12},{5,13},{6,14},{7,15},{8,0},{9,1},... | collective-permute-start | bytes 884744 | tf_op jit(solution)/shard_map/ppermute | solution.py:848
  214.8 8.5 %collective-permute-start.22 = (bf16[2,768,384]{2,1,0:T(8,128)(2,1)}, bf16[2,768,384]{2,1,0:T(8,128)(2,1)S(1)}, u32[]{:S(2)}, u32[]{:S(2)}) collective-permute-start(bf16[2,768,384]{2,1,0:T(8,128)(2,1)} %get-tuple-element.166), channel_id=1, source_target_pairs={{0,1},{1,0},{2,3},{3,2},{4,5},{5,4},{6,7},{7,6},{8,9},{9,8},{10,11... | collective-permute-start | bytes 3538952 | tf_op jit(solution)/shard_map/ppermute | solution.py:848
  214.9 15.4 %collective-permute-start.23 = (bf16[4,112,576]{2,1,0:T(8,128)(2,1)S(1)}, bf16[4,112,576]{2,1,0:T(8,128)(2,1)S(1)}, u32[]{:S(2)}, u32[]{:S(2)}) collective-permute-start(bf16[4,112,576]{2,1,0:T(8,128)(2,1)S(1)} %copy-done.33), channel_id=1, source_target_pairs={{0,4},{1,5},{2,6},{3,7},{4,0},{5,1},{6,2},{7,3},{8,12},{9,13},{10,... | collective-permute-start | bytes 1548296 | tf_op jit(solution)/shard_map/ppermute | solution.py:848
  215.2 15.1 %collective-permute-start.24 = (bf16[4,112,576]{2,1,0:T(8,128)(2,1)S(1)}, bf16[4,112,576]{2,1,0:T(8,128)(2,1)S(1)}, u32[]{:S(2)}, u32[]{:S(2)}) collective-permute-start(bf16[4,112,576]{2,1,0:T(8,128)(2,1)S(1)} %copy-done.32), channel_id=1, source_target_pairs={{0,8},{1,9},{2,10},{3,11},{4,12},{5,13},{6,14},{7,15},{8,0},{9,1},... | collective-permute-start | bytes 1548296 | tf_op jit(solution)/shard_map/ppermute | solution.py:848
  227.2 18.6 %collective-permute-start.26 = (bf16[768,384]{1,0:T(8,128)(2,1)S(1)}, bf16[768,384]{1,0:T(8,128)(2,1)S(1)}, u32[]{:S(2)}, u32[]{:S(2)}) collective-permute-start(bf16[768,384]{1,0:T(8,128)(2,1)S(1)} %get-tuple-element.176), channel_id=1, source_target_pairs={{0,2},{1,3},{2,0},{3,1},{4,6},{5,7},{6,4},{7,5},{8,10},{9,11},{10,... | collective-permute-start | bytes 1769480 | tf_op jit(solution)/shard_map/ppermute | solution.py:848
  227.8 15.7 %collective-permute-start.25 = (bf16[2,96,768]{2,1,0:T(8,128)(2,1)S(1)}, bf16[2,96,768]{2,1,0:T(8,128)(2,1)S(1)}, u32[]{:S(2)}, u32[]{:S(2)}) collective-permute-start(bf16[2,96,768]{2,1,0:T(8,128)(2,1)S(1)} %get-tuple-element.159), channel_id=1, source_target_pairs={{0,16},{1,17},{2,18},{3,19},{4,20},{5,21},{6,22},{7,23},{8,24},{9,... | collective-permute-start | bytes 884744 | tf_op jit(solution)/shard_map/ppermute | solution.py:848
  245.1 9.8 %collective-permute-start.28 = (bf16[2,112,576]{2,1,0:T(8,128)(2,1)S(1)}, bf16[2,112,576]{2,1,0:T(8,128)(2,1)S(1)}, u32[]{:S(2)}, u32[]{:S(2)}) collective-permute-start(bf16[2,112,576]{2,1,0:T(8,128)(2,1)S(1)} %get-tuple-element.180), channel_id=1, source_target_pairs={{0,4},{1,5},{2,6},{3,7},{4,0},{5,1},{6,2},{7,3},{8,12},{9,13},{10,... | collective-permute-start | bytes 774152 | tf_op jit(solution)/shard_map/ppermute | solution.py:848
  247.2 12.1 %collective-permute-start.29 = (bf16[4,96,384]{2,1,0:T(8,128)(2,1)S(1)}, bf16[4,96,384]{2,1,0:T(8,128)(2,1)S(1)}, u32[]{:S(2)}, u32[]{:S(2)}) collective-permute-start(bf16[4,96,384]{2,1,0:T(8,128)(2,1)S(1)} %get-tuple-element.177), channel_id=1, source_target_pairs={{0,4},{1,5},{2,6},{3,7},{4,0},{5,1},{6,2},{7,3},{8,12},{9,13},{10,... | collective-permute-start | bytes 884744 | tf_op jit(solution)/shard_map/ppermute | solution.py:848
  248.6 13.1 %collective-permute-start.30 = (bf16[2,96,768]{2,1,0:T(8,128)(2,1)S(1)}, bf16[2,96,768]{2,1,0:T(8,128)(2,1)S(1)}, u32[]{:S(2)}, u32[]{:S(2)}) collective-permute-start(bf16[2,96,768]{2,1,0:T(8,128)(2,1)S(1)} %shard_map.338.refs_0_), channel_id=1, source_target_pairs={{0,1},{1,0},{2,3},{3,2},{4,5},{5,4},{6,7},{7,6},{8,9},{9,8},{10,11... | collective-permute-start | bytes 884744 | tf_op jit(solution)/shard_map/ppermute | solution.py:848
  251.7 10.1 %collective-permute-start.32 = (bf16[2,96,768]{2,1,0:T(8,128)(2,1)S(1)}, bf16[2,96,768]{2,1,0:T(8,128)(2,1)S(1)}, u32[]{:S(2)}, u32[]{:S(2)}) collective-permute-start(bf16[2,96,768]{2,1,0:T(8,128)(2,1)S(1)} %collective-permute-done.31.refs_2_), channel_id=1, source_target_pairs={{0,1},{1,0},{2,3},{3,2},{4,5},{5,4},{6,7},{7,6},{8,9},{9,8},{10,11... | collective-permute-start | bytes 884744 | tf_op jit(solution)/shard_map/ppermute | solution.py:848
  255.5 13.2 %collective-permute-start.34 = (bf16[2,112,576]{2,1,0:T(8,128)(2,1)S(1)}, bf16[2,112,576]{2,1,0:T(8,128)(2,1)S(1)}, u32[]{:S(2)}, u32[]{:S(2)}) collective-permute-start(bf16[2,112,576]{2,1,0:T(8,128)(2,1)S(1)} %get-tuple-element.183), channel_id=1, source_target_pairs={{0,16},{1,17},{2,18},{3,19},{4,20},{5,21},{6,22},{7,23},{8,24},{9,... | collective-permute-start | bytes 774152 | tf_op jit(solution)/shard_map/ppermute | solution.py:848
  270.2 11.7 %collective-permute-start.36 = (bf16[2,112,576]{2,1,0:T(8,128)(2,1)S(1)}, bf16[2,112,576]{2,1,0:T(8,128)(2,1)S(1)}, u32[]{:S(2)}, u32[]{:S(2)}) collective-permute-start(bf16[2,112,576]{2,1,0:T(8,128)(2,1)S(1)} %shard_map.344.refs_0_), channel_id=1, source_target_pairs={{0,1},{1,0},{2,3},{3,2},{4,5},{5,4},{6,7},{7,6},{8,9},{9,8},{10,11... | collective-permute-start | bytes 774152 | tf_op jit(solution)/shard_map/ppermute | solution.py:848
  (47 other events, 364.7 us)
